TPU v7x, 256 devices: a whole 4x4x8 slice. The times are simulated.
256 devices in a mesh: dp: 32 (over z, y), mp: 8 (over x, core).
Axes of the slice: x: 4, y: 4, z: 8, core: 2. Of those that a mesh axis runs over, the one named last changes fastest.
Arguments:
- queries: bfloat16 [12288, 4096], P('dp', 'mp'), may hold values from -16 to 16
- states: bfloat16 [256, 128, 896], P('dp', 'mp'), may hold values from -6 to 6
- key_weight: bfloat16 [896, 4096], P(None, 'mp'), may hold values from -0.1875 to 0.1875
- value_weight: bfloat16 [896, 4096], P(None, 'mp'), may hold values from -0.1875 to 0.1875
- nbr_shard: int32 [192, 2], P('dp'), may hold values from 0 to 31, all different within a row; in each aligned block of 6 rows (0 to 5, 6 to 11, ...) at most 2 rows name the same one
- nbr_row: int32 [192, 2], P('dp'), may hold values from 0 to 7
- out_grad: bfloat16 [12288, 4096], P('dp', 'mp'), may hold values from -6 to 6
Outputs:
- attended: bfloat16 [12288, 4096], P('dp', 'mp')
- query_grad: bfloat16 [12288, 4096], P('dp', 'mp')
- state_grad: float32 [256, 128, 896], P('dp', 'mp')
- key_weight_grad: float32 [896, 4096], P(None, 'mp')
- value_weight_grad: float32 [896, 4096], P(None, 'mp')
Inputs may be any that keep to these rules, and one draw needn't show every extreme that they name: `nbr_shard`: the 2 neighbours of a span lie on different shards; among the 6 spans of one device at most 2 neighbours lie on one shard, and some shard takes exactly 2 of them.
All inputs are finite; a program needn't handle non-finite values.
Results may differ from a plain program's by a relative error of at most 0.02.
Values may be sent and summed in bfloat16 or wider, within the bound.
A program may use at most 128 MiB of HBM per device.

v0:
```python
import jax
import jax.numpy as jnp
from jax import lax
from jax.sharding import PartitionSpec as P

D = 4096
H = 32


def body(queries, states, key_weight, value_weight, nbr_shard, nbr_row, out_grad):
    shards = lax.axis_size("dp")
    groups = lax.axis_size("mp")
    spans, neighbours = nbr_shard.shape
    pair_count = spans * neighbours
    tokens, local_width = queries.shape
    span_len = tokens // spans
    slab_len = states.shape[1]
    enc_width = states.shape[2]
    full_len = slab_len * groups
    head_dim = D // H
    local_heads = local_width // head_dim
    capacity = max(2, (pair_count + shards - 1) // shards)
    slot_count = shards * capacity
    owners = nbr_shard.reshape(pair_count)
    row_index = nbr_row.reshape(pair_count)
    owner_hot = (owners[:, None] == jnp.arange(shards, dtype=jnp.int32)[None, :]).astype(jnp.int32)
    earlier = (jnp.arange(pair_count)[:, None] > jnp.arange(pair_count)[None, :]).astype(jnp.int32)
    before_count = jnp.dot(earlier, owner_hot)
    ranking = jnp.sum(before_count * owner_hot, axis=1)
    slot_index = owners * capacity + ranking
    matched = slot_index[:, None] == jnp.arange(slot_count, dtype=jnp.int32)[None, :]
    asked_rows = jnp.sum(jnp.where(matched, row_index[:, None], 0), axis=0).reshape(
        shards, capacity
    )
    incoming = lax.all_to_all(asked_rows, "dp", split_axis=0, concat_axis=0, tiled=True)
    slab_rows = jnp.take(states, incoming, axis=0)
    sent_back = lax.all_to_all(slab_rows, "dp", split_axis=0, concat_axis=0, tiled=True)
    flat_recv = sent_back.reshape(slot_count, slab_len, enc_width)
    picked = jnp.take(flat_recv, slot_index, axis=0)
    gathered = lax.all_gather(picked, "mp", axis=1, tiled=True)
    rows_all = gathered.reshape(pair_count * full_len, enc_width)
    key_rows = jnp.dot(rows_all, key_weight, preferred_element_type=jnp.float32).astype(
        jnp.bfloat16
    )
    value_rows = jnp.dot(rows_all, value_weight, preferred_element_type=jnp.float32).astype(
        jnp.bfloat16
    )
    key_heads = key_rows.reshape(spans, neighbours * full_len, local_heads, head_dim)
    value_heads = value_rows.reshape(spans, neighbours * full_len, local_heads, head_dim)
    query_heads = queries.reshape(spans, span_len, local_heads, head_dim)
    grad_heads = out_grad.reshape(spans, span_len, local_heads, head_dim)
    score_scale = 1.0 / head_dim**0.5
    scores = (
        jnp.einsum("cqhd,ckhd->chqk", query_heads, key_heads, preferred_element_type=jnp.float32)
        * score_scale
    )
    probs = jax.nn.softmax(scores, axis=-1)
    probs_low = probs.astype(jnp.bfloat16)
    attended = jnp.einsum(
        "chqk,ckhd->cqhd", probs_low, value_heads, preferred_element_type=jnp.float32
    )
    attended = attended.astype(jnp.bfloat16).reshape(tokens, local_width)
    prob_grad = jnp.einsum(
        "cqhd,ckhd->chqk", grad_heads, value_heads, preferred_element_type=jnp.float32
    )
    row_dot = jnp.sum(probs * prob_grad, axis=-1, keepdims=True)
    score_grad = (score_scale * probs * (prob_grad - row_dot)).astype(jnp.bfloat16)
    query_grad = jnp.einsum(
        "chqk,ckhd->cqhd", score_grad, key_heads, preferred_element_type=jnp.float32
    )
    query_grad = query_grad.astype(jnp.bfloat16).reshape(tokens, local_width)
    key_grad = jnp.einsum(
        "chqk,cqhd->ckhd", score_grad, query_heads, preferred_element_type=jnp.float32
    )
    key_grad = key_grad.astype(jnp.bfloat16).reshape(pair_count * full_len, local_width)
    value_grad = jnp.einsum(
        "chqk,cqhd->ckhd", probs_low, grad_heads, preferred_element_type=jnp.float32
    )
    value_grad = value_grad.astype(jnp.bfloat16).reshape(pair_count * full_len, local_width)
    state_term = lax.dot_general(
        key_grad, key_weight, (((1,), (1,)), ((), ())), preferred_element_type=jnp.float32
    )
    state_term = state_term + lax.dot_general(
        value_grad, value_weight, (((1,), (1,)), ((), ())), preferred_element_type=jnp.float32
    )
    state_term = state_term.reshape(pair_count, full_len, enc_width)
    pair_grad = lax.psum_scatter(
        state_term.astype(jnp.bfloat16), "mp", scatter_dimension=1, tiled=True
    )
    outgoing = jnp.einsum(
        "ps,pte->ste", matched.astype(jnp.bfloat16), pair_grad, preferred_element_type=jnp.float32
    )
    outgoing = outgoing.astype(jnp.bfloat16).reshape(shards, capacity, slab_len, enc_width)
    returned = lax.all_to_all(outgoing, "dp", split_axis=0, concat_axis=0, tiled=True).reshape(
        slot_count, slab_len, enc_width
    )
    owned_hot = (
        incoming.reshape(slot_count)[None, :]
        == jnp.arange(states.shape[0], dtype=jnp.int32)[:, None]
    ).astype(jnp.bfloat16)
    state_total = jnp.einsum("rs,ste->rte", owned_hot, returned, preferred_element_type=jnp.float32)
    key_wgrad = lax.dot_general(
        rows_all, key_grad, (((0,), (0,)), ((), ())), preferred_element_type=jnp.float32
    )
    value_wgrad = lax.dot_general(
        rows_all, value_grad, (((0,), (0,)), ((), ())), preferred_element_type=jnp.float32
    )
    key_total, value_total = lax.psum((key_wgrad, value_wgrad), "dp")
    return (attended, query_grad, state_total, key_total, value_total)


def solution(mesh):
    placed = (
        P("dp", "mp"),
        P("dp", "mp", None),
        P(None, "mp"),
        P(None, "mp"),
        P("dp", None),
        P("dp", None),
        P("dp", "mp"),
    )
    return jax.shard_map(
        body,
        mesh=mesh,
        in_specs=placed,
        out_specs=(P("dp", "mp"), P("dp", "mp"), P("dp", "mp", None), P(None, "mp"), P(None, "mp")),
        check_vma=False,
    )
```

profile of v0, /device:TPU:2, one launch (start us, length us, event | category | flops | bytes accessed | tf_op | source)
XLA Modules:
  0.0 404.2 jit_solution(16408007588507303971)
XLA Ops:
  7.2 0.8 copy.51
  8.0 0.1 broadcast_in_dim.44
  8.1 0.8 copy.50
  8.9 0.1 reshape.136
  9.0 0.3 fusion.41
  9.3 0.1 select_reduce_fusion
  9.4 0.1 all_to_all.16
  9.5 21.0 %all_to_all.25 = s32[32,1,2]{2,1,0:T(1,128)S(1)} all-to-all(s32[32,1,2]{2,1,0:T(1,128)S(1)} %bitcast.103), channel_id=1, replica_groups=mesh['dp'=32,'mp'=8] {'dp'}, dimensions={0} | all-to-all | bytes 512 | tf_op jit(solution)/shard_map/all_to_all | solution.py:35
  30.5 0.1 copy.53
  30.6 0.1 copy.54
  30.7 0.1 copy.56
  30.8 0.1 reshape.151
  30.9 1.8 gather_fusion
  32.7 1.5 broadcast_select_fusion
  34.2 4.1 %all-to-all-start.1 = ((bf16[32,2,16,896]{3,2,1,0:T(8,128)(2,1)}), bf16[32,2,16,896]{3,2,1,0:T(8,128)(2,1)S(1)}, u32[]{:S(2)}, u32[]{:S(2)}) async-start(bf16[32,2,16,896]{3,2,1,0:T(8,128)(2,1)} %broadcast_select_fusion), calls=%async_computation.1 | async-start | bytes 3670016 | tf_op jit(solution)/shard_map/all_to_all | solution.py:37
  38.4 0.1 copy.57
  38.5 0.1 mul.41
  38.6 43.8 %all-to-all-done.1 = bf16[32,2,16,896]{3,2,1,0:T(8,128)(2,1)S(1)} async-done(((bf16[32,2,16,896]{3,2,1,0:T(8,128)(2,1)}), bf16[32,2,16,896]{3,2,1,0:T(8,128)(2,1)S(1)}, u32[]{:S(2)}, u32[]{:S(2)}) %all-to-all-start.1) | async-done | bytes 1835040 | tf_op jit(solution)/shard_map/all_to_all | solution.py:37
  82.4 0.6 gather_fusion.1
  83.0 0.8 broadcast_select_fusion.1
  83.9 0.0 reduce-scatter.2.cloned.1.call-start
  83.9 0.1 reshape.141
  84.0 0.1 reshape.143
  84.1 24.6 %all-gather.2.cloned.1.call-done = bf16[12,128,896]{2,1,0:T(8,128)(2,1)} async-done(((bf16[12,16,896]{2,1,0:T(8,128)(2,1)}), bf16[12,128,896]{2,1,0:T(8,128)(2,1)}) %all-gather.2.cloned.1.call-update) | async-done | bytes 2752528 | tf_op jit(solution)/shard_map/all_gather | solution.py:40
  108.8 4.7 %convolution_convert_fusion = bf16[1536,512]{1,0:T(8,128)(2,1)} fusion(bf16[1536,896]{1,0:T(8,128)(2,1)} %bitcast.104, bf16[896,512]{1,0:T(8,128)(2,1)S(1)} %copy-done), kind=kOutput, calls=%fused_computation.4 | convolution fusion | flops 1410072576 | bytes 5242880 | tf_op jit(solution)/shard_map/dot_general | solution.py:42
  113.5 2.4 reshape.140
  115.9 5.0 %convolution_convert_fusion.1 = bf16[1536,512]{1,0:T(8,128)(2,1)} fusion(bf16[1536,896]{1,0:T(8,128)(2,1)} %bitcast.105, bf16[896,512]{1,0:T(8,128)(2,1)} %param.10), kind=kOutput, calls=%fused_computation.5 | convolution fusion | flops 1410072576 | bytes 5242880 | tf_op jit(solution)/shard_map/dot_general | solution.py:45
  120.8 3.5 reshape.139
  124.3 0.7 convolution_multiply_fusion
  125.0 1.7 fusion.65
  126.7 5.8 %fusion.14 = bf16[6,256,4,128]{3,1,2,0:T(8,128)(2,1)} fusion(bf16[6,64,4,128]{3,2,1,0:T(4,128)(2,1)S(1)} %reshape.143, f32[6,4,64]{2,1,0:T(4,128)S(1)} %get-tuple-element.24, f32[6,4,256,64]{2,3,1,0:T(8,128)} %copy-done.2), kind=kOutput, calls=%fused_computation.26 | convolution fusion | flops 102631168 | bytes 3545088 | tf_op jit(solution)/shard_map/chqk,cqhd->ckhd/dot_general | solution.py:76
  132.5 2.8 copy.69
  135.3 1.2 fusion.9
  136.5 0.5 fusion.11
  137.0 0.5 copy-done.6
  137.5 0.6 fusion.13
  138.1 1.2 copy.67
  139.4 1.8 fusion.7
  141.2 1.9 add_convert_fusion
  143.2 3.4 copy.70
  146.6 5.1 %fusion.5 = f32[896,512]{1,0:T(8,128)} fusion(bf16[1536,896]{1,0:T(8,128)(2,1)} %bitcast.106, bf16[192,8,4,128]{3,2,1,0:T(4,128)(2,1)} %bitcast.100), kind=kOutput, calls=%fused_computation.14 | convolution fusion | flops 1409286144 | bytes 6160384 | tf_op jit(solution)/shard_map/dot_general | solution.py:102
  151.7 32.5 %reduce-scatter.2.cloned.1.call-done = bf16[12,16,896]{2,0,1:T(8,128)(2,1)} async-done(((bf16[12,128,896]{2,0,1:T(8,128)(2,1)}), bf16[12,16,896]{2,0,1:T(8,128)(2,1)}) %reduce-scatter.2.cloned.1.call-update) | async-done | bytes 344080 | tf_op jit(solution)/shard_map/reduce_scatter | solution.py:87
  184.2 3.0 convolution_convert_fusion.2
  187.2 4.8 %reshape.147 = bf16[32,2,16,896]{3,1,0,2:T(2,128)(2,1)} reshape(bf16[64,16,896]{2,0,1:T(8,128)(2,1)} %convolution_convert_fusion.2) | data formatting | bytes 3670016 | tf_op jit(solution)/shard_map/reshape | solution.py:93
  192.0 4.0 copy.71
  195.9 9.8 %all-to-all-start.2 = ((bf16[32,2,16,896]{3,1,2,0:T(2,128)(2,1)}), bf16[32,2,16,896]{3,1,2,0:T(2,128)(2,1)}, u32[]{:S(2)}, u32[]{:S(2)}) async-start(bf16[32,2,16,896]{3,1,2,0:T(2,128)(2,1)} %copy.71), calls=%async_computation.3 | async-start | bytes 3670016 | tf_op jit(solution)/shard_map/all_to_all | solution.py:94
  205.8 0.3 all-reduce.3.cloned.1.call-start
  206.0 5.1 %fusion.2 = f32[896,512]{1,0:T(8,128)} fusion(bf16[1536,896]{1,0:T(8,128)(2,1)} %bitcast.107, bf16[192,8,4,128]{3,2,1,0:T(4,128)(2,1)} %bitcast.97), kind=kOutput, calls=%fused_computation.11 | convolution fusion | flops 1409286144 | bytes 6160384 | tf_op jit(solution)/shard_map/dot_general | solution.py:105
  211.1 0.5 broadcast.109
  211.7 0.7 reduce.3
  212.4 0.1 eq.47
  212.5 0.4 fusion.38
  212.8 0.3 copy.65
  213.2 4.6 %fusion.35 = bf16[6,64,4,128]{3,1,2,0:T(8,128)(2,1)S(1)} fusion(bf16[6,256,4,128]{3,2,1,0:T(4,128)(2,1)} %reshape.139, f32[6,4,64]{2,1,0:T(4,128)S(1)} %get-tuple-element.24, f32[6,4,256,64]{2,3,1,0:T(8,128)} %copy-done.2), kind=kOutput, calls=%fused_computation.42 | convolution fusion | flops 102041344 | bytes 3545088 | tf_op jit(solution)/shard_map/chqk,ckhd->cqhd/dot_general | solution.py:59
  217.8 0.3 copy.61
  218.1 1.0 copy_bitcast_fusion
  219.1 41.8 %all-to-all-done.2 = bf16[32,2,16,896]{3,1,2,0:T(2,128)(2,1)} async-done(((bf16[32,2,16,896]{3,1,2,0:T(2,128)(2,1)}), bf16[32,2,16,896]{3,1,2,0:T(2,128)(2,1)}, u32[]{:S(2)}, u32[]{:S(2)}) %all-to-all-start.2) | async-done | bytes 1835040 | tf_op jit(solution)/shard_map/all_to_all | solution.py:94
  260.9 4.4 %copy.72 = bf16[32,2,16,896]{3,1,0,2:T(2,128)(2,1)} copy(bf16[32,2,16,896]{3,1,2,0:T(2,128)(2,1)} %all-to-all-done.2) | data formatting | bytes 3670016 | tf_op jit(solution)/shard_map/all_to_all | solution.py:94
  265.3 4.1 %reshape.148 = bf16[64,16,896]{2,0,1:T(8,128)(2,1)S(1)} reshape(bf16[32,2,16,896]{3,1,0,2:T(2,128)(2,1)} %copy.72) | data formatting | bytes 3670016 | tf_op jit(solution)/shard_map/reshape | solution.py:94
  269.4 0.3 fusion.53
  269.8 0.9 copy.73
  270.7 122.7 %all-reduce.3.cloned.1.call-done = (f32[896,512]{1,0:T(8,128)}, f32[896,512]{1,0:T(8,128)}) async-done(((f32[896,512]{1,0:T(8,128)}, f32[896,512]{1,0:T(8,128)}), (f32[896,512]{1,0:T(8,128)}, f32[896,512]{1,0:T(8,128)})) %all-reduce.3.cloned.1.call-update) | async-done | bytes 3670032 | tf_op jit(solution)/shard_map/psum | solution.py:108
  393.4 3.0 copy.126
  396.4 1.2 copy.127
  (38 shorter events, 0.2 us)
Async XLA Ops:
  7.2 101.6 %copy-start = (bf16[896,512]{1,0:T(8,128)(2,1)S(1)}, bf16[896,512]{1,0:T(8,128)(2,1)}, u32[]{:S(2)}) copy-start(bf16[896,512]{1,0:T(8,128)(2,1)} %param.9) | copy-start | bytes 2752516
  34.2 4.2 %copy-start.13 = (s32[6,2]{0,1:T(2,128)S(1)}, s32[6,2]{0,1:T(2,128)}, u32[]{:S(2)}) copy-start(s32[6,2]{0,1:T(2,128)} %param.11) | copy-start | bytes 148
  34.2 48.2 %all-to-all-start.1 = ((bf16[32,2,16,896]{3,2,1,0:T(8,128)(2,1)}), bf16[32,2,16,896]{3,2,1,0:T(8,128)(2,1)S(1)}, u32[]{:S(2)}, u32[]{:S(2)}) async-start(bf16[32,2,16,896]{3,2,1,0:T(8,128)(2,1)} %broadcast_select_fusion), calls=%async_computation.1 | async-start | bytes 3670016 | tf_op jit(solution)/shard_map/all_to_all | solution.py:37
  38.3 45.6 %copy-start.11 = (bf16[384,512]{1,0:T(8,128)(2,1)S(1)}, bf16[384,512]{1,0:T(8,128)(2,1)}, u32[]{:S(2)}) copy-start(bf16[384,512]{1,0:T(8,128)(2,1)} %param.7) | copy-start | bytes 1179652
  38.3 70.5 %all-gather.2.cloned.1.call-start = ((), (), s32[]{:S(2)}) async-start(), calls=%async_computation.4 | async-start | bytes 3096576 | tf_op jit(solution)/shard_map/all_gather | solution.py:40
  83.0 1.0 copy-start.12
  83.9 100.3 %reduce-scatter.2.cloned.1.call-start = ((), (), s32[]{:S(2)}) async-start(), calls=%async_computation.5 | async-start | bytes 4128768 | tf_op jit(solution)/shard_map/reduce_scatter | solution.py:87
  84.0 40.3 %copy-start.5 = (bf16[6,64,4,128]{3,2,1,0:T(4,128)(2,1)}, bf16[6,64,4,128]{3,2,1,0:T(4,128)(2,1)S(1)}, u32[]{:S(2)}) copy-start(bf16[6,64,4,128]{3,2,1,0:T(4,128)(2,1)S(1)} %reshape.141) | copy-start | bytes 1179652
  125.0 1.7 copy-start.2
  132.5 2.8 copy-start.3
  132.5 2.8 copy-start.8
  135.3 6.0 %copy-start.4 = (bf16[6,256,4,128]{3,2,1,0:T(4,128)(2,1)}, bf16[6,256,4,128]{3,2,1,0:T(4,128)(2,1)S(1)}, u32[]{:S(2)}) copy-start(bf16[6,256,4,128]{3,2,1,0:T(4,128)(2,1)S(1)} %copy.69) | copy-start | bytes 4718596
  136.5 1.0 copy-start.6
  139.4 1.9 copy-start.9
  139.4 1.9 copy-start.10
  195.9 65.0 %all-to-all-start.2 = ((bf16[32,2,16,896]{3,1,2,0:T(2,128)(2,1)}), bf16[32,2,16,896]{3,1,2,0:T(2,128)(2,1)}, u32[]{:S(2)}, u32[]{:S(2)}) async-start(bf16[32,2,16,896]{3,1,2,0:T(2,128)(2,1)} %copy.71), calls=%async_computation.3 | async-start | bytes 3670016 | tf_op jit(solution)/shard_map/all_to_all | solution.py:94
  205.8 187.6 %all-reduce.3.cloned.1.call-start = ((), (), s32[]{:S(2)}) async-start(), calls=%async_computation.6 | async-start | bytes 7340032 | tf_op jit(solution)/shard_map/psum | solution.py:108
  393.4 3.0 copy-start.7
  393.4 4.3 %copy-start.1 = (bf16[896,512]{1,0:T(8,128)(2,1)S(1)}, bf16[896,512]{1,0:T(8,128)(2,1)}, u32[]{:S(2)}) copy-start(bf16[896,512]{1,0:T(8,128)(2,1)} %param.9) | copy-start | bytes 2752516
Sparse Core Ops, SparseCore 0:
  84.0 24.7 all-gather.1
  146.7 37.4 reduce-scatter.1
  211.3 182.0 all-reduce.2
where the time goes:
time: 405 us; the launch traced here: 404 us
  waiting for transfers between devices  265 us (65%)
  local copies, waits for them, and re-layouts  43.4 us (11%)
  matrix products  40.6 us (10%)
  blocking collectives  21 us (5%)
  starting transfers between devices  14.3 us (4%)
  between operations  14.1 us (3%)
  other arithmetic  5.31 us (1%)
    psum x1, waiting for transfers between devices, body(): key_total, value_total = lax.psum((key_wgrad, value_wgrad), 'dp')  123 us
    all_to_all x1, waiting for transfers between devices, body(): lax.all_to_all(slab_rows, 'dp', split_axis=0, concat_axis=0, tiled=True)  43.8 us
    all_to_all x1, waiting for transfers between devices, body(): lax.all_to_all(outgoing, 'dp', split_axis=0, concat_axis=0, tiled=True)  41.8 us
    reduce_scatter x1, waiting for transfers between devices, body(): lax.psum_scatter(state_term.astype(jnp.bfloat16), 'mp', scatter_dimension...  32.5 us
    all_gather x1, waiting for transfers between devices, body(): gathered = lax.all_gather(picked, 'mp', axis=1, tiled=True)  24.6 us
    all_to_all x1, blocking collectives, body(): lax.all_to_all(asked_rows, 'dp', split_axis=0, concat_axis=0, tiled=True)  21 us
    all_to_all x1, starting transfers between devices, body(): lax.all_to_all(outgoing, 'dp', split_axis=0, concat_axis=0, tiled=True)  9.83 us
    reshape x2, local copies, waits for them, and re-layouts, body(): outgoing.astype(jnp.bfloat16).reshape(shards, capacity, slab_len, enc_width)  8.78 us
  transfers between devices with their start and end apart: 5, of which 5 were waited for; matrix products, arithmetic and copies ran while one was open for 7% of the time, Pallas kernels for 0%

commit v1 on v0

v1 whole, which is shorter than its diff:
```python
import functools

import jax
import jax.numpy as jnp
from jax import lax
from jax.experimental import pallas as pl
from jax.experimental.pallas import tpu as pltpu
from jax.sharding import PartitionSpec as P

D = 4096
H = 32
HD = 128
NZ, NY, NX = 8, 4, 4
GROUPS = 8
SLOTS = 12
HALF = SLOTS // 2
ROWS = 8
TOK = 16
E = 896
CHUNKS = ((0, 512), (512, 384))
VMEM_LIMIT = 56 * 1024 * 1024
BF16 = jnp.bfloat16
F32 = jnp.float32


class Place:
    def __init__(self):
        dp, mp = lax.axis_index("dp"), lax.axis_index("mp")
        self.dp, self.mp = dp, mp
        self.z, self.y = dp // NY, lax.rem(dp, NY)
        self.x, self.core = mp // 2, lax.rem(mp, 2)

    def zi(self, k):
        return lax.rem(self.z + (k + NZ), NZ)

    def yi(self, k):
        return lax.rem(self.y + (k + NY), NY)

    def xi(self, k):
        return lax.rem(self.x + (k + NX), NX)

    def at_z(self, k):
        return (self.zi(k) * NY + self.y, self.mp)

    def at_y(self, k):
        return (self.z * NY + self.yi(k), self.mp)

    def at_x(self, k):
        return (self.dp, self.xi(k) * 2 + self.core)

    def sibling(self):
        return (self.dp, self.x * 2 + (1 - self.core))

    def partners(self):
        return [
            self.at_z(1), self.at_z(-1), self.at_y(1), self.at_y(-1), self.at_y(2),
            self.at_x(1), self.at_x(-1), self.sibling(),
        ]


class Net:
    def __init__(self, send_sems, recv_sems, local_sems):
        self.send_sems, self.recv_sems, self.local_sems = send_sems, recv_sems, local_sems
        self.sent = []
        self.locals = 0

    def send(self, src, dst, device):
        number = len(self.sent)
        copy = pltpu.make_async_remote_copy(
            src_ref=src,
            dst_ref=dst,
            send_sem=self.send_sems.at[number],
            recv_sem=self.recv_sems.at[number],
            device_id=device,
            device_id_type=pl.DeviceIdType.MESH,
        )
        copy.start()
        self.sent.append(copy)
        return copy

    def local(self, src, dst):
        copy = pltpu.make_async_copy(src, dst, self.local_sems.at[self.locals])
        copy.start()
        self.locals += 1
        return copy

    def finish(self):
        for copy in self.sent:
            copy.wait_send()


def greet(place):
    barrier = pltpu.get_barrier_semaphore()
    partners = place.partners()
    for device in partners:
        pl.semaphore_signal(barrier, inc=1, device_id=device, device_id_type=pl.DeviceIdType.MESH)
    pl.semaphore_wait(barrier, len(partners))


def run_chains(chains):
    live = list(chains)
    turn = 0
    while live:
        rest = []
        for first, chain in live:
            if turn >= first:
                try:
                    next(chain)
                except StopIteration:
                    continue
            rest.append((first, chain))
        live = rest
        turn += 1


def part(ref, bounds):
    first, count = bounds
    return ref.at[pl.ds(first, count)]


def ring_gather(net, n, right, left, slot, halves, landed=None):
    half_r, half_l = halves
    whole = (half_r[0], half_r[1] + half_l[1])
    far = n // 2
    for step in range(1, far + 1):
        piece_r = half_r if step == far else whole
        piece_l = half_l if step == far else whole
        block_r, block_l = part(slot(1 - step), piece_r), part(slot(step - 1), piece_l)
        to_right = net.send(block_r, block_r, right)
        to_left = net.send(block_l, block_l, left)
        yield
        to_right.wait_recv()
        if landed is not None:
            landed(part(slot(-step), piece_r))
        to_left.wait_recv()
        if landed is not None:
            landed(part(slot(step), piece_l))


def add_into(target, *others):
    total = target[...].astype(F32)
    for other in others:
        total = total + other[...].astype(F32)
    target[...] = total.astype(target.dtype)


def ring_scatter(net, n, right, left, total, prepare, from_left, from_right, halves):
    half_r, half_l = halves
    whole = (half_r[0], half_r[1] + half_l[1])
    far = n // 2
    prepare(far)
    to_right = [net.send(part(total(far), half_r), part(from_left(0), half_r), right)]
    to_left = [net.send(part(total(far), half_l), part(from_right(0), half_l), left)]
    for step in range(1, far):
        k = far - step
        prepare(k)
        prepare(-k)
        early_r, early_l = [], []
        if step == 1:
            early_r.append(net.send(part(total(k), half_l), part(from_left(step), half_l), right))
            early_l.append(net.send(part(total(-k), half_r), part(from_right(step), half_r), left))
        piece_r = half_r if step == 1 else whole
        piece_l = half_l if step == 1 else whole
        yield
        for copy in to_right:
            copy.wait_recv()
        add_into(part(total(k), piece_r), part(from_left(step - 1), piece_r))
        to_right = early_r + [net.send(part(total(k), piece_r), part(from_left(step), piece_r), right)]
        for copy in to_left:
            copy.wait_recv()
        add_into(part(total(-k), piece_l), part(from_right(step - 1), piece_l))
        to_left = early_l + [net.send(part(total(-k), piece_l), part(from_right(step), piece_l), left)]
    prepare(0)
    yield
    for copy in to_right + to_left:
        copy.wait_recv()
    add_into(total(0), from_left(far - 1), from_right(far - 1))


SLOT_HALVES = ((0, HALF), (HALF, HALF))
ROW_HALVES = ((0, ROWS // 2), (ROWS // 2, ROWS // 2))


FWD_COPIES = 96
FWD_LOCALS = 16


def fwd_kernel(meta_in, states, *refs):
    count = len(CHUNKS)
    outs, refs = refs[:count], refs[count:]
    meta_out, refs = refs[0], refs[1:]
    per_chunk = [refs[6 * i:6 * i + 6] for i in range(count)]
    meta_v, meta_s, send_sems, recv_sems, local_sems = refs[6 * count:]
    place = Place()
    net = Net(send_sems, recv_sems, local_sems)
    own_meta = net.local(meta_in, meta_v.at[place.y])
    loads = []
    for (first, width), bufs in zip(CHUNKS, per_chunk):
        loads.append(net.local(states.at[:, :, pl.ds(first, width)], bufs[0].at[place.z]))
    greet(place)

    def meta_chain():
        copies = [net.send(meta_in, meta_v.at[place.y], place.at_y(k)) for k in (1, -1, 2)]
        yield
        own_meta.wait()
        for copy in copies:
            copy.wait_recv()
        to_smem = net.local(meta_v, meta_s)
        to_out = net.local(meta_v, meta_out)
        to_smem.wait()
        to_out.wait()

    def chunk_chain(i):
        zbuf, send1, recv1, send2, recv2, rows = per_chunk[i]
        first, width = CHUNKS[i]
        loads[i].wait()
        yield from ring_gather(
            net, NZ, place.at_z(1), place.at_z(-1), lambda k: zbuf.at[place.zi(k)], ROW_HALVES
        )
        yield
        y, right, left = place.y, place.at_y(1), place.at_y(-1)

        def held(k, j):
            dest = place.yi(k)
            entry = meta_s[dest, 0, j]
            return zbuf[entry // ROWS, lax.rem(entry, ROWS)]

        def column(k, j):
            return meta_s[place.yi(k), 1, j]

        for j in range(HALF):
            send1[0, j] = held(2, j)
            send1[1, j] = held(2, j + HALF)
        one_r = net.send(send1.at[0], recv1.at[0], right)
        one_l = net.send(send1.at[1], recv1.at[1], left)
        for j in range(HALF):
            send2[0, j + HALF] = held(1, j + HALF)
            send2[1, j] = held(-1, j)
        two_r = net.send(send2.at[0, pl.ds(HALF, HALF)], recv2.at[0, pl.ds(HALF, HALF)], right)
        two_l = net.send(send2.at[1, pl.ds(0, HALF)], recv2.at[1, pl.ds(0, HALF)], left)
        yield
        one_r.wait_recv()
        for j in range(HALF):
            send2[0, j] = lax.select(column(1, j) == y, held(1, j), recv1[0, j])
        three_r = net.send(send2.at[0, pl.ds(0, HALF)], recv2.at[0, pl.ds(0, HALF)], right)
        one_l.wait_recv()
        for j in range(HALF):
            send2[1, j + HALF] = lax.select(column(-1, j + HALF) == y, held(-1, j + HALF), recv1[1, j])
        three_l = net.send(send2.at[1, pl.ds(HALF, HALF)], recv2.at[1, pl.ds(HALF, HALF)], left)
        yield
        for copy in (two_r, two_l, three_r, three_l):
            copy.wait_recv()
        mp = place.mp
        for j in range(SLOTS):
            own_column = column(0, j)
            by_left = own_column == place.yi(-1)
            if j < HALF:
                by_left = jnp.logical_or(by_left, own_column == place.yi(2))
            other = lax.select(by_left, recv2[0, j], recv2[1, j])
            rows[j, mp] = lax.select(own_column == y, held(0, j), other)
        across = []

        def landed(block):
            across.append(net.send(block, block, place.sibling()))

        def slot(k):
            return rows.at[:, place.xi(k) * 2 + place.core]

        landed(slot(0))
        yield from ring_gather(net, NX, place.at_x(1), place.at_x(-1), slot, SLOT_HALVES, landed)
        yield
        for copy in across:
            copy.wait_recv()
        done = net.local(rows, outs[i])
        yield
        done.wait()

    run_chains([(0, meta_chain())] + [(2 * i, chunk_chain(i)) for i in range(count)])
    net.finish()


def forward(meta, states):
    scratch = []
    for _, width in CHUNKS:
        scratch += [
            pltpu.VMEM((NZ, ROWS, TOK, width), BF16),
            pltpu.VMEM((2, HALF, TOK, width), BF16),
            pltpu.VMEM((2, HALF, TOK, width), BF16),
            pltpu.VMEM((2, SLOTS, TOK, width), BF16),
            pltpu.VMEM((2, SLOTS, TOK, width), BF16),
            pltpu.VMEM((SLOTS, GROUPS, TOK, width), BF16),
        ]
    scratch += [
        pltpu.VMEM((NY, 8, 128), jnp.int32),
        pltpu.SMEM((NY, 8, 128), jnp.int32),
        pltpu.SemaphoreType.DMA((FWD_COPIES,)),
        pltpu.SemaphoreType.DMA((FWD_COPIES,)),
        pltpu.SemaphoreType.DMA((FWD_LOCALS,)),
    ]
    return pl.pallas_call(
        fwd_kernel,
        out_shape=[jax.ShapeDtypeStruct((SLOTS, GROUPS, TOK, w), BF16) for _, w in CHUNKS]
        + [jax.ShapeDtypeStruct((NY, 8, 128), jnp.int32)],
        in_specs=[pl.BlockSpec(memory_space=pltpu.VMEM), pl.BlockSpec(memory_space=pl.ANY)],
        out_specs=[pl.BlockSpec(memory_space=pl.ANY)] * (len(CHUNKS) + 1),
        scratch_shapes=scratch,
        compiler_params=pltpu.CompilerParams(
            collective_id=0, has_side_effects=True, vmem_limit_bytes=VMEM_LIMIT
        ),
        name="gather_slabs",
    )(meta, states)


SPAN_LEN = 64
STEP_SPANS = 2
LOCAL = 512
HEADS = LOCAL // HD


def mm(a, b, dims):
    return lax.dot_general(a, b, (dims, ((), ())), preferred_element_type=F32)


def attend_kernel(q, g, kw, vw, *refs):
    count = len(CHUNKS)
    row_refs, refs = refs[:count], refs[count:]
    att, qg = refs[0], refs[1]
    state_outs, refs = refs[2:2 + count], refs[2 + count:]
    kgrad, vgrad, total = refs
    step = pl.program_id(0)
    tokens = STEP_SPANS * 2 * 128
    scale = 1.0 / HD**0.5
    rows = [ref[...].reshape(tokens, w) for ref, (_, w) in zip(row_refs, CHUNKS)]

    def project(weight):
        out = None
        for piece, (first, width) in zip(rows, CHUNKS):
            term = mm(piece, weight[pl.ds(first, width), :], ((1,), (0,)))
            out = term if out is None else out + term
        return out.astype(BF16)

    keys, values = project(kw), project(vw)
    key_parts, value_parts = [], []
    for c in range(STEP_SPANS):
        key_heads, value_heads = [], []
        for h in range(HEADS):
            cols = slice(h * HD, (h + 1) * HD)
            span = slice(c * SPAN_LEN, (c + 1) * SPAN_LEN)
            span_rows = slice(c * 256, (c + 1) * 256)
            qh, gh = q[span, cols], g[span, cols]
            kh, vh = keys[span_rows, cols], values[span_rows, cols]
            scores = mm(qh, kh, ((1,), (1,))) * scale
            top = jnp.max(scores, axis=-1, keepdims=True)
            grown = jnp.exp(scores - top)
            probs = grown / jnp.sum(grown, axis=-1, keepdims=True)
            low = probs.astype(BF16)
            att[span, cols] = mm(low, vh, ((1,), (0,))).astype(BF16)
            pgrad = mm(gh, vh, ((1,), (1,)))
            dot = jnp.sum(probs * pgrad, axis=-1, keepdims=True)
            sgrad = (scale * probs * (pgrad - dot)).astype(BF16)
            qg[span, cols] = mm(sgrad, kh, ((1,), (0,))).astype(BF16)
            key_heads.append(mm(sgrad, qh, ((0,), (0,))).astype(BF16))
            value_heads.append(mm(low, gh, ((0,), (0,))).astype(BF16))
        key_parts.append(jnp.concatenate(key_heads, axis=1))
        value_parts.append(jnp.concatenate(value_heads, axis=1))
    kg, vg = jnp.concatenate(key_parts, axis=0), jnp.concatenate(value_parts, axis=0)
    for ref, (first, width) in zip(state_outs, CHUNKS):
        piece = pl.ds(first, width)
        term = mm(kg, kw[piece, :], ((1,), (1,))) + mm(vg, vw[piece, :], ((1,), (1,)))
        ref[...] = term.astype(BF16).reshape(ref.shape)

    @pl.when(step == 0)
    def _():
        total[...] = jnp.zeros_like(total)

    for piece, (first, width) in zip(rows, CHUNKS):
        at = pl.ds(first, width)
        total[at, pl.ds(0, LOCAL)] += mm(piece, kg, ((0,), (0,)))
        total[at, pl.ds(LOCAL, LOCAL)] += mm(piece, vg, ((0,), (0,)))

    @pl.when(step == pl.num_programs(0) - 1)
    def _():
        for z in range(NZ):
            for h in range(HEADS):
                at = pl.ds(z * WROWS, WROWS)
                kgrad[z, h] = total[at, pl.ds(h * HD, HD)].astype(BF16)
                vgrad[z, h] = total[at, pl.ds(LOCAL + h * HD, HD)].astype(BF16)


WROWS = E // NZ


def attend(queries, out_grad, key_weight, value_weight, rows):
    steps = queries.shape[0] // (STEP_SPANS * SPAN_LEN)
    slots = STEP_SPANS * 2
    token_spec = pl.BlockSpec((STEP_SPANS * SPAN_LEN, LOCAL), lambda i: (i, 0))
    weight_spec = pl.BlockSpec((E, LOCAL), lambda i: (0, 0))
    row_specs = [pl.BlockSpec((slots, GROUPS, TOK, w), lambda i: (i, 0, 0, 0)) for _, w in CHUNKS]
    grad_spec = pl.BlockSpec((NZ, HEADS, WROWS, HD), lambda i: (0, 0, 0, 0))
    grad_shape = jax.ShapeDtypeStruct((NZ, HEADS, WROWS, HD), BF16)
    return pl.pallas_call(
        attend_kernel,
        grid=(steps,),
        out_shape=[jax.ShapeDtypeStruct(queries.shape, BF16)] * 2
        + [jax.ShapeDtypeStruct((SLOTS, GROUPS, TOK, w), BF16) for _, w in CHUNKS]
        + [grad_shape] * 2,
        in_specs=[token_spec, token_spec, weight_spec, weight_spec] + row_specs,
        out_specs=[token_spec, token_spec] + row_specs + [grad_spec] * 2,
        scratch_shapes=[pltpu.VMEM((E, 2 * LOCAL), F32)],
        compiler_params=pltpu.CompilerParams(vmem_limit_bytes=VMEM_LIMIT),
        name="attend",
    )(queries, out_grad, key_weight, value_weight, *rows)


BWD_COPIES = 160
BWD_LOCALS = 24
HEAD_HALVES = ((0, HEADS // 2), (HEADS // 2, HEADS // 2))
ZBLOCK_HALVES = ((0, NZ // 2), (NZ // 2, NZ // 2))
WROW_HALVES = ((0, 64), (64, WROWS - 64))


def bwd_kernel(meta, *refs):
    count = len(CHUNKS)
    terms, refs = refs[:count], refs[count:]
    kgrad, vgrad, state_out, kout, vout = refs[:5]
    refs = refs[5:]
    per_chunk = [refs[8 * i:8 * i + 8] for i in range(count)]
    refs = refs[8 * count:]
    (kw, kfl, kfr, ky, kmine, kres, vw, vyl, vyr, vzl, vzr, vres, send_sems, recv_sems, local_sems) = refs
    place = Place()
    net = Net(send_sems, recv_sems, local_sems)
    order = (2, 1, -1, 0)
    loads = []
    for i in range(count):
        mine = per_chunk[i][0]
        loads.append(
            [net.local(terms[i].at[:, place.xi(k) * 2 + place.core], mine.at[n]) for n, k in enumerate(order)]
        )
    load_k, load_v = net.local(kgrad, kw), net.local(vgrad, vw)
    greet(place)

    def nothing(k):
        pass

    def state_chain(i):
        mine, theirs, xl, xr, ybuf, part_buf, zl, zr = per_chunk[i]
        first, width = CHUNKS[i]
        crossing = [
            net.send(terms[i].at[:, place.xi(k) * 2 + (1 - place.core)], theirs.at[n], place.sibling())
            for n, k in enumerate(order)
        ]
        yield

        def prepare_x(k):
            n = order.index(k)
            loads[i][n].wait()
            crossing[n].wait_recv()
            add_into(mine.at[n], theirs.at[n])

        yield from ring_scatter(
            net, NX, place.at_x(1), place.at_x(-1), lambda k: mine.at[order.index(k)], prepare_x,
            lambda s: xl.at[s], lambda s: xr.at[s], SLOT_HALVES,
        )
        ybuf[place.y] = mine[3]
        yield from ring_gather(
            net, NY, place.at_y(1), place.at_y(-1), lambda k: ybuf.at[place.yi(k)], SLOT_HALVES
        )

        def prepare_z(k):
            shard = place.zi(k) * NY + place.y
            where = (k + NZ) % NZ
            named = [
                (d, meta[d, 2, shard * 2 + r], meta[d, 3, shard * 2 + r]) for d in range(NY) for r in range(2)
            ]
            for row in range(ROWS):
                total = None
                for d, slot, slot_row in named:
                    weight = jnp.where(slot_row == row, 1.0, 0.0).astype(F32)
                    term = ybuf[d, slot].astype(F32) * weight
                    total = term if total is None else total + term
                part_buf[where, row] = total.astype(BF16)

        yield from ring_scatter(
            net, NZ, place.at_z(1), place.at_z(-1), lambda k: part_buf.at[(k + NZ) % NZ], prepare_z,
            lambda s: zl.at[s], lambda s: zr.at[s], ROW_HALVES,
        )
        state_out[:, :, pl.ds(first, width)] = part_buf[0].astype(F32)

    def key_chain():
        load_k.wait()
        yield from ring_scatter(
            net, NZ, place.at_z(1), place.at_z(-1), lambda k: kw.at[place.zi(k)], nothing,
            lambda s: kfl.at[s], lambda s: kfr.at[s], HEAD_HALVES,
        )
        own = kw.at[place.z]
        copies = [net.send(own.at[place.yi(k)], ky.at[n], place.at_y(k)) for n, k in enumerate((1, -1, 2))]
        yield
        for copy in copies:
            copy.wait_recv()
        kmine[...] = own[place.y]
        add_into(kmine, ky.at[0], ky.at[1], ky.at[2])
        spot = kres.at[place.z, place.y]
        copies = [net.send(kmine, spot, place.at_y(k)) for k in (1, -1, 2)]
        kres[place.z, place.y] = kmine[...]
        yield
        for copy in copies:
            copy.wait_recv()
        yield from ring_gather(
            net, NZ, place.at_z(1), place.at_z(-1), lambda k: kres.at[place.zi(k)], HEAD_HALVES
        )
        done = net.local(kres, kout)
        yield
        done.wait()

    def value_chain():
        load_v.wait()
        yield from ring_scatter(
            net, NY, place.at_y(1), place.at_y(-1), lambda k: vw.at[:, place.yi(k)], nothing,
            lambda s: vyl.at[s], lambda s: vyr.at[s], ZBLOCK_HALVES,
        )
        yield from ring_scatter(
            net, NZ, place.at_z(1), place.at_z(-1), lambda k: vw.at[place.zi(k), place.y], nothing,
            lambda s: vzl.at[s], lambda s: vzr.at[s], WROW_HALVES,
        )
        vres[place.z, place.y] = vw[place.z, place.y]
        yield from ring_gather(
            net, NZ, place.at_z(1), place.at_z(-1), lambda k: vres.at[place.zi(k), place.y], WROW_HALVES
        )
        yield from ring_gather(
            net, NY, place.at_y(1), place.at_y(-1), lambda k: vres.at[:, place.yi(k)], ZBLOCK_HALVES
        )
        done = net.local(vres, vout)
        yield
        done.wait()

    run_chains(
        [(2 * i, state_chain(i)) for i in range(count)] + [(0, key_chain()), (0, value_chain())]
    )
    net.finish()


def backward(meta, terms, kgrad, vgrad):
    scratch = []
    for _, width in CHUNKS:
        scratch += [
            pltpu.VMEM((NX, SLOTS, TOK, width), BF16),
            pltpu.VMEM((NX, SLOTS, TOK, width), BF16),
            pltpu.VMEM((2, SLOTS, TOK, width), BF16),
            pltpu.VMEM((2, SLOTS, TOK, width), BF16),
            pltpu.VMEM((NY, SLOTS, TOK, width), BF16),
            pltpu.VMEM((NZ, ROWS, TOK, width), BF16),
            pltpu.VMEM((NZ // 2, ROWS, TOK, width), BF16),
            pltpu.VMEM((NZ // 2, ROWS, TOK, width), BF16),
        ]
    scratch += [
        pltpu.VMEM((NZ, HEADS, WROWS, HD), BF16),
        pltpu.VMEM((NZ // 2, HEADS, WROWS, HD), BF16),
        pltpu.VMEM((NZ // 2, HEADS, WROWS, HD), BF16),
        pltpu.VMEM((3, WROWS, HD), BF16),
        pltpu.VMEM((WROWS, HD), BF16),
        pltpu.VMEM((NZ, HEADS, WROWS, HD), BF16),
        pltpu.VMEM((NZ, HEADS, WROWS, HD), BF16),
        pltpu.VMEM((NY // 2, NZ, WROWS, HD), BF16),
        pltpu.VMEM((NY // 2, NZ, WROWS, HD), BF16),
        pltpu.VMEM((NZ // 2, WROWS, HD), BF16),
        pltpu.VMEM((NZ // 2, WROWS, HD), BF16),
        pltpu.VMEM((NZ, HEADS, WROWS, HD), BF16),
        pltpu.SemaphoreType.DMA((BWD_COPIES,)),
        pltpu.SemaphoreType.DMA((BWD_COPIES,)),
        pltpu.SemaphoreType.DMA((BWD_LOCALS,)),
    ]
    anywhere = pl.BlockSpec(memory_space=pl.ANY)
    grad_shape = jax.ShapeDtypeStruct((NZ, HEADS, WROWS, HD), BF16)
    return pl.pallas_call(
        bwd_kernel,
        out_shape=[jax.ShapeDtypeStruct((ROWS, TOK, E), F32), grad_shape, grad_shape],
        in_specs=[pl.BlockSpec(memory_space=pltpu.SMEM)] + [anywhere] * (len(CHUNKS) + 2),
        out_specs=[pl.BlockSpec(memory_space=pltpu.VMEM), anywhere, anywhere],
        scratch_shapes=scratch,
        compiler_params=pltpu.CompilerParams(
            collective_id=1, has_side_effects=True, vmem_limit_bytes=VMEM_LIMIT
        ),
        name="sum_grads",
    )(meta, *terms, kgrad, vgrad)


def describe(nbr_shard, nbr_row):
    owners, rows = nbr_shard.reshape(SLOTS), nbr_row.reshape(SLOTS)
    entry = (owners // NY) * ROWS + rows
    column = lax.rem(owners, NY)
    slots = jnp.arange(SLOTS, dtype=jnp.int32)
    same = jnp.logical_and(owners[:, None] == owners[None, :], slots[:, None] > slots[None, :])
    key = owners * 2 + jnp.sum(same.astype(jnp.int32), axis=1)
    hit = key[:, None] == jnp.arange(128, dtype=jnp.int32)[None, :]
    slot_of = jnp.sum(jnp.where(hit, slots[:, None], 0), axis=0)
    row_of = jnp.sum(jnp.where(hit, rows[:, None] + 1, 0), axis=0) - 1
    pad = (0, 128 - SLOTS)
    blank = jnp.zeros((128,), jnp.int32)
    return jnp.stack([jnp.pad(entry, pad), jnp.pad(column, pad), slot_of, row_of] + [blank] * 4)


def unpack(grad):
    return grad.transpose(0, 2, 1, 3).reshape(E, LOCAL).astype(F32)


def body(queries, states, key_weight, value_weight, nbr_shard, nbr_row, out_grad):
    *rows, metas = forward(describe(nbr_shard, nbr_row), states)
    attended, query_grad, *rest = attend(queries, out_grad, key_weight, value_weight, rows)
    terms, kgrad, vgrad = rest[:-2], rest[-2], rest[-1]
    state_total, ktotal, vtotal = backward(metas, terms, kgrad, vgrad)
    return attended, query_grad, state_total, unpack(ktotal), unpack(vtotal)


def solution(mesh):
    placed = (
        P("dp", "mp"),
        P("dp", "mp", None),
        P(None, "mp"),
        P(None, "mp"),
        P("dp", None),
        P("dp", None),
        P("dp", "mp"),
    )
    return jax.shard_map(
        body,
        mesh=mesh,
        in_specs=placed,
        out_specs=(P("dp", "mp"), P("dp", "mp"), P("dp", "mp", None), P(None, "mp"), P(None, "mp")),
        check_vma=False,
    )
```

time: 405 us -> 169 us (0.42)
  waiting for transfers between devices: 265 us -> 0 us
  Pallas kernels: 0 us -> 158 us
  matrix products: 40.6 us -> 0 us
  local copies, waits for them, and re-layouts: 43.4 us -> 7.31 us
  blocking collectives: 21 us -> 0 us
  starting transfers between devices: 14.3 us -> 0 us
  between operations: 14.1 us -> 0.71 us
    pallas_call x0 -> x3, Pallas kernels: none -> 158 us  [the longest x1 72.2 us: backward(): pl.pallas_call(bwd_kernel, out_shape=[jax.ShapeDtypeStruct((ROWS, TOK, E)...]
    psum x1 -> x0, waiting for transfers between devices: 123 us -> none  [body(): key_total, value_total = lax.psum((key_wgrad, value_wgrad), 'dp')]
    all_to_all x2 -> x0, waiting for transfers between devices: 85.6 us -> none  [the longest x1 43.8 us: body(): lax.all_to_all(slab_rows, 'dp', split_axis=0, concat_axis=0, tiled=True)]
    dot_general x15 -> x0, matrix products: 40.6 us -> none  [the longest x1 5.83 us: body(): jnp.einsum('chqk,cqhd->ckhd', probs_low, grad_heads, preferred_element_ty...]
    reduce_scatter x1 -> x0, waiting for transfers between devices: 32.5 us -> none  [body(): lax.psum_scatter(state_term.astype(jnp.bfloat16), 'mp', scatter_dimension...]
    all_gather x1 -> x0, waiting for transfers between devices: 24.6 us -> none  [body(): gathered = lax.all_gather(picked, 'mp', axis=1, tiled=True)]
    all_to_all x1 -> x0, blocking collectives: 21 us -> none  [body(): lax.all_to_all(asked_rows, 'dp', split_axis=0, concat_axis=0, tiled=True)]
    reshape x9 -> x2, local copies, waits for them, and re-layouts: 20 us -> 0.16 us  [describe(): owners, rows = (nbr_shard.reshape(SLOTS), nbr_row.reshape(SLOTS))]
  transfers between devices with their start and end apart: 5 -> 0, of which waited for: 5 -> 0; matrix products, arithmetic and copies ran while one was open for 7% -> 0% of each run, Pallas kernels for 0% -> 0%
where the time goes in v1:
time: 169 us; the launch traced here: 168 us
  Pallas kernels  158 us (93%)
  local copies, waits for them, and re-layouts  7.31 us (4%)
  other arithmetic  1.76 us (1%)
    pallas_call x1, Pallas kernels, backward(): pl.pallas_call(bwd_kernel, out_shape=[jax.ShapeDtypeStruct((ROWS, TOK, E)...  72.2 us
    pallas_call x1, Pallas kernels, forward(): pl.pallas_call(fwd_kernel, out_shape=[jax.ShapeDtypeStruct((SLOTS, GROUPS...  60.4 us
    pallas_call x1, Pallas kernels, attend(): pl.pallas_call(attend_kernel, grid=(steps,), out_shape=[jax.ShapeDtypeStr...  25.8 us
    unnamed x9, local copies, waits for them, and re-layouts  5.11 us

profile of v1, /device:TPU:2, one launch (start us, length us, event | category | flops | bytes accessed | tf_op | source)
XLA Modules:
  0.0 168.2 jit_solution(15919448812910236659)
XLA Ops:
  0.6 0.8 copy.18
  1.4 0.1 reshape.48
  1.5 0.2 convert_reduce_fusion
  1.7 0.8 copy.19
  2.4 0.1 reshape.49
  2.5 0.1 select_reduce_fusion
  2.6 0.6 stack.20.meta_in
  3.2 60.4 %gather_slabs.1 = (bf16[12,8,16,512]{3,2,1,0:T(8,128)(2,1)}, bf16[12,8,16,384]{3,2,1,0:T(8,128)(2,1)}, s32[4,8,128]{2,1,0:T(8,128)}) custom-call(s32[8,128]{1,0:T(8,128)} %stack.20.meta_in, bf16[8,16,896]{2,1,0:T(8,128)(2,1)} %states.1), custom_call_target="tpu_custom_call" | custom-call | tf_op jit(solution)/shard_map/gather_slabs/pallas_call | solution.py:300
  63.7 25.8 %attend.1 = (bf16[384,512]{1,0:T(8,128)(2,1)}, bf16[384,512]{1,0:T(8,128)(2,1)}, bf16[12,8,16,512]{3,2,1,0:T(8,128)(2,1)}, bf16[12,8,16,384]{3,2,1,0:T(8,128)(2,...) custom-call(bf16[384,512]{1,0:T(8,128)(2,1)} %q.1, bf16[384,512]{1,0:T(8,128)(2,1)} %g.1, ...), custom_call_target="tpu_custom_call" | custom-call | tf_op jit(solution)/shard_map/attend/pallas_call | solution.py:401
  89.5 72.2 %sum_grads.1 = (f32[8,16,896]{2,1,0:T(8,128)}, bf16[8,4,112,128]{3,2,1,0:T(8,128)(2,1)}, bf16[8,4,112,128]{3,2,1,0:T(8,128)(2,1)}) custom-call(s32[4,8,128]{2,1,0:T(8,128)} %get-tuple-element.21.meta, bf16[12,8,16,512]{3,2,1,0:T(8,128)(2,1)} %get-tuple-element.22.refs_0_, bf16[12,8,16,384]{3,2,1,0:T(8,128)(2,1)} %get-tuple-element.23.refs_1_, ...), custom_call_target="tpu_custom_call" | custom-call | tf_op jit(solution)/shard_map/sum_grads/pallas_call | solution.py:574
  161.7 1.3 convert_bitcast_fusion.1
  163.1 0.7 copy.20
  163.8 0.0 copy-start
  163.8 1.4 copy.27
  165.2 0.1 copy-done
  165.2 0.1 convert_bitcast_fusion
  165.4 0.7 copy.21
  166.1 0.0 copy-start.1
  166.1 1.4 copy.26
  167.5 0.0 copy-done.1
  167.5 0.8 copy.29
  (4 shorter events, 0.0 us)
Async XLA Ops:
  163.8 1.4 copy-start
  166.1 1.4 copy-start.1

commit v2 on v0

v2 whole, which is shorter than its diff:
```python
import jax
import jax.numpy as jnp
from jax import lax
from jax.experimental import pallas as pl
from jax.experimental.pallas import tpu as pltpu
from jax.sharding import PartitionSpec as P

D = 4096
H = 32
HD = 128
NZ, NY, NX = 8, 4, 4
GROUPS = 8
SLOTS = 12
HALF = SLOTS // 2
ROWS = 8
TOK = 16
E = 896
VMEM_LIMIT = 56 * 1024 * 1024
BF16 = jnp.bfloat16
F32 = jnp.float32


class Place:
    def __init__(self):
        dp, mp = lax.axis_index("dp"), lax.axis_index("mp")
        self.dp, self.mp = dp, mp
        self.z, self.y = dp // NY, lax.rem(dp, NY)
        self.x, self.core = mp // 2, lax.rem(mp, 2)

    def zi(self, k):
        return lax.rem(self.z + (k + NZ), NZ)

    def yi(self, k):
        return lax.rem(self.y + (k + NY), NY)

    def xi(self, k):
        return lax.rem(self.x + (k + NX), NX)

    def at_z(self, k):
        return (self.zi(k) * NY + self.y, self.mp)

    def at_y(self, k):
        return (self.z * NY + self.yi(k), self.mp)

    def at_x(self, k):
        return (self.dp, self.xi(k) * 2 + self.core)

    def sibling(self):
        return (self.dp, self.x * 2 + (1 - self.core))

    def partners(self):
        return [
            self.at_z(1), self.at_z(-1), self.at_y(1), self.at_y(-1), self.at_y(2),
            self.at_x(1), self.at_x(-1), self.at_x(2), self.sibling(),
        ]


class Net:
    def __init__(self, send_sems, recv_sems, local_sems):
        self.send_sems, self.recv_sems, self.local_sems = send_sems, recv_sems, local_sems
        self.sent = []
        self.locals = 0

    def send(self, src, dst, device):
        number = len(self.sent)
        copy = pltpu.make_async_remote_copy(
            src_ref=src,
            dst_ref=dst,
            send_sem=self.send_sems.at[number],
            recv_sem=self.recv_sems.at[number],
            device_id=device,
            device_id_type=pl.DeviceIdType.MESH,
        )
        copy.start()
        self.sent.append(copy)
        return copy

    def local(self, src, dst):
        copy = pltpu.make_async_copy(src, dst, self.local_sems.at[self.locals])
        copy.start()
        self.locals += 1
        return copy

    def finish(self):
        for copy in self.sent:
            copy.wait_send()


def greet(place):
    barrier = pltpu.get_barrier_semaphore()
    partners = place.partners()
    for device in partners:
        pl.semaphore_signal(barrier, inc=1, device_id=device, device_id_type=pl.DeviceIdType.MESH)
    pl.semaphore_wait(barrier, len(partners))


def part(ref, bounds):
    first, count = bounds
    return ref.at[pl.ds(first, count)]


def ring_gather(net, n, right, left, slot, halves, landed=None):
    half_r, half_l = halves
    whole = (half_r[0], half_r[1] + half_l[1])
    far = n // 2
    for step in range(1, far + 1):
        piece_r = half_r if step == far else whole
        piece_l = half_l if step == far else whole
        block_r, block_l = part(slot(1 - step), piece_r), part(slot(step - 1), piece_l)
        to_right = net.send(block_r, block_r, right)
        to_left = net.send(block_l, block_l, left)
        yield
        to_right.wait_recv()
        if landed is not None:
            landed(part(slot(-step), piece_r))
        to_left.wait_recv()
        if landed is not None:
            landed(part(slot(step), piece_l))


def add_into(target, *others):
    total = target[...].astype(F32)
    for other in others:
        total = total + other[...].astype(F32)
    target[...] = total.astype(target.dtype)


def ring_scatter(net, n, right, left, total, prepare, from_left, from_right, halves):
    half_r, half_l = halves
    whole = (half_r[0], half_r[1] + half_l[1])
    far = n // 2
    prepare(far)
    to_right = [net.send(part(total(far), half_r), part(from_left(0), half_r), right)]
    to_left = [net.send(part(total(far), half_l), part(from_right(0), half_l), left)]
    for step in range(1, far):
        k = far - step
        prepare(k)
        prepare(-k)
        early_r, early_l = [], []
        if step == 1:
            early_r.append(net.send(part(total(k), half_l), part(from_left(step), half_l), right))
            early_l.append(net.send(part(total(-k), half_r), part(from_right(step), half_r), left))
        piece_r = half_r if step == 1 else whole
        piece_l = half_l if step == 1 else whole
        yield
        for copy in to_right:
            copy.wait_recv()
        add_into(part(total(k), piece_r), part(from_left(step - 1), piece_r))
        to_right = early_r + [net.send(part(total(k), piece_r), part(from_left(step), piece_r), right)]
        for copy in to_left:
            copy.wait_recv()
        add_into(part(total(-k), piece_l), part(from_right(step - 1), piece_l))
        to_left = early_l + [net.send(part(total(-k), piece_l), part(from_right(step), piece_l), left)]
    prepare(0)
    yield
    for copy in to_right + to_left:
        copy.wait_recv()
    add_into(total(0), from_left(far - 1), from_right(far - 1))


ROW_HALVES = ((0, ROWS // 2), (ROWS // 2, ROWS // 2))
SPAN_LEN = 64
LOCAL = 512
PARTS = 3
SPART = SLOTS // PARTS
PROWS = GROUPS * SPART * TOK
WROWS = E // NZ
UNITS = 4
UNIT_HALVES = ((0, UNITS // 2), (UNITS // 2, UNITS // 2))
ZBLOCK_HALVES = ((0, NZ // 2), (NZ // 2, NZ // 2))
WROW_HALVES = ((0, 64), (64, WROWS - 64))
COPIES = 160
LOCALS = 32
AROUND = (1, -1, 2)


def mm(a, b, dims):
    return lax.dot_general(a, b, (dims, ((), ())), preferred_element_type=F32)


def kernel(
    meta_in, states, queries, out_grad, key_weight, value_weight,
    att, qg, state_out, kout, vout,
    meta_v, meta_s, q, g, weights, zbuf, ysend, yrecv, rows, rows_t, grads, terms, theirs, xrecv,
    ybuf, share, zl, zr, wgrad, wfl, wfr, wy, wres, vyl, vyr, vzl, vzr, vres,
    send_sems, recv_sems, local_sems,
):
    place = Place()
    net = Net(send_sems, recv_sems, local_sems)
    y, mp = place.y, place.mp
    load_states = net.local(states, zbuf.at[place.z])
    own_meta = net.local(meta_in, meta_v.at[y])
    loads = []
    half = LOCAL // 2
    for i in range(2):
        from_cols = pl.ds(i * half, half)
        loads.append(net.local(key_weight.at[:, from_cols], weights.at[i, :, pl.ds(0, half)]))
        loads.append(net.local(value_weight.at[:, from_cols], weights.at[i, :, pl.ds(half, half)]))
    loads.append(net.local(queries, q))
    loads.append(net.local(out_grad, g))
    greet(place)

    meta_copies = [net.send(meta_in, meta_v.at[y], place.at_y(k)) for k in AROUND]
    load_states.wait()
    for turn, _ in enumerate(
        ring_gather(net, NZ, place.at_z(1), place.at_z(-1), lambda k: zbuf.at[place.zi(k)], ROW_HALVES)
    ):
        if turn == 1:
            own_meta.wait()
            for copy in meta_copies:
                copy.wait_recv()
            to_smem = net.local(meta_v, meta_s)
    to_smem.wait()

    def fetch(p):
        at = pl.ds(p * SPART, SPART)

        def held(k, j):
            entry = meta_s[place.yi(k), 0, j]
            return zbuf[entry // ROWS, lax.rem(entry, ROWS)]

        copies = []
        for n, k in enumerate(AROUND):
            for j in range(SPART):
                ysend[p, n, j] = held(k, p * SPART + j)
            copies.append(net.send(ysend.at[p, n], yrecv.at[p, n], place.at_y(k)))
        yield
        for copy in copies:
            copy.wait_recv()
        for j in range(SPART):
            column = meta_s[y, 1, p * SPART + j]
            value = lax.select(column == place.yi(-1), yrecv[p, 0, j], yrecv[p, 1, j])
            value = lax.select(column == place.yi(2), yrecv[p, 2, j], value)
            rows[mp, p * SPART + j] = lax.select(column == y, held(0, p * SPART + j), value)

        def block(k):
            return rows.at[place.xi(k) * 2 + place.core, at]

        across = [net.send(block(0), block(0), place.sibling())]
        copies = [net.send(block(0), block(0), place.at_x(k)) for k in AROUND]
        yield
        for copy, k in zip(copies, (-1, 1, 2)):
            copy.wait_recv()
            across.append(net.send(block(k), block(k), place.sibling()))
        yield
        for copy in across:
            copy.wait_recv()

    def attend(p, i):
        scale = 1.0 / HD**0.5
        at = pl.ds(p * SPART, SPART)
        part_rows = rows[:, at].reshape(PROWS, E)
        if i == 0:
            rows_t[:, pl.ds(p * PROWS, PROWS)] = part_rows.T
        both = mm(part_rows, weights[i], ((1,), (0,))).astype(BF16).reshape(GROUPS, SPART, TOK, LOCAL)
        for c in range(SPART // 2):
            span_both = both[:, 2 * c:2 * c + 2].reshape(2 * GROUPS * TOK, LOCAL)
            span = pl.ds((p * (SPART // 2) + c) * SPAN_LEN, SPAN_LEN)
            for h in range(2):
                cols = pl.ds((2 * i + h) * HD, HD)
                qh, gh = q[span, cols], g[span, cols]
                kh = span_both[:, h * HD:(h + 1) * HD]
                vh = span_both[:, half + h * HD:half + (h + 1) * HD]
                scores = mm(qh, kh, ((1,), (1,))) * scale
                top = jnp.max(scores, axis=-1, keepdims=True)
                grown = jnp.exp(scores - top)
                probs = grown / jnp.sum(grown, axis=-1, keepdims=True)
                low = probs.astype(BF16)
                att[span, cols] = mm(low, vh, ((1,), (0,))).astype(BF16)
                pgrad = mm(gh, vh, ((1,), (1,)))
                dot = jnp.sum(probs * pgrad, axis=-1, keepdims=True)
                sgrad = (scale * probs * (pgrad - dot)).astype(BF16)
                qg[span, cols] = mm(sgrad, kh, ((1,), (0,))).astype(BF16)
                shape = (GROUPS, 2, TOK, HD)
                pair = pl.ds(2 * c, 2)
                grads[i, p, :, pair, :, pl.ds(h * HD, HD)] = (
                    mm(sgrad, qh, ((0,), (0,))).astype(BF16).reshape(shape)
                )
                grads[i, p, :, pair, :, pl.ds(half + h * HD, HD)] = (
                    mm(low, gh, ((0,), (0,))).astype(BF16).reshape(shape)
                )

    def slab_term(p):
        total = None
        for i in range(2):
            term = mm(grads[i, p].reshape(PROWS, LOCAL), weights[i], ((1,), (1,)))
            total = term if total is None else total + term
        terms[:, pl.ds(p * SPART, SPART)] = total.astype(BF16).reshape(GROUPS, SPART, TOK, E)

    def weight_term(i):
        total = mm(rows_t[...], grads[i].reshape(PARTS * PROWS, LOCAL), ((1,), (0,))).astype(BF16)
        for z in range(NZ):
            for u in range(UNITS):
                wgrad[i, z, u] = total[z * WROWS:(z + 1) * WROWS, u * HD:(u + 1) * HD]

    def give_back(p):
        at = pl.ds(p * SPART, SPART)
        order = AROUND + (0,)
        copies = [
            net.send(terms.at[place.xi(k) * 2 + (1 - place.core), at], theirs.at[p, n], place.sibling())
            for n, k in enumerate(order)
        ]
        yield
        crossing = []
        for n, k in enumerate(order):
            copies[n].wait_recv()
            block = terms.at[place.xi(k) * 2 + place.core, at]
            add_into(block, theirs.at[p, n])
            if k != 0:
                crossing.append(net.send(block, xrecv.at[p, n], place.at_x(k)))
        yield
        for copy in crossing:
            copy.wait_recv()
        total = terms[mp, at].astype(F32)
        for n in range(3):
            total = total + xrecv[p, n].astype(F32)
        ybuf[y, at] = total.astype(BF16)
        copies = [net.send(ybuf.at[y, at], ybuf.at[y, at], place.at_y(k)) for k in AROUND]
        yield
        for copy in copies:
            copy.wait_recv()

    def nothing(k):
        pass

    def sum_slabs():
        def prepare(k):
            shard = place.zi(k) * NY + y
            named = [
                (d, meta_s[d, 2, shard * 2 + r], meta_s[d, 3, shard * 2 + r]) for d in range(NY) for r in range(2)
            ]
            for row in range(ROWS):
                total = None
                for d, slot, slot_row in named:
                    weight = jnp.where(slot_row == row, 1.0, 0.0).astype(F32)
                    term = ybuf[d, slot].astype(F32) * weight
                    total = term if total is None else total + term
                share[(k + NZ) % NZ, row] = total.astype(BF16)

        yield from ring_scatter(
            net, NZ, place.at_z(1), place.at_z(-1), lambda k: share.at[(k + NZ) % NZ], prepare,
            lambda s: zl.at[s], lambda s: zr.at[s], ROW_HALVES,
        )
        state_out[...] = share[0].astype(F32)

    def result(res, i):
        return [
            net.local(res.at[:, u], out.at[:, :, pl.ds((2 * i + u % 2) * HD, HD)])
            for u, out in enumerate((kout, kout, vout, vout))
        ]

    def sum_z_first():
        total = wgrad.at[0]
        yield from ring_scatter(
            net, NZ, place.at_z(1), place.at_z(-1), lambda k: total.at[place.zi(k)], nothing,
            lambda s: wfl.at[s], lambda s: wfr.at[s], UNIT_HALVES,
        )
        wy[y] = total[place.z]
        copies = [net.send(wy.at[y], wy.at[y], place.at_y(k)) for k in AROUND]
        yield
        for copy in copies:
            copy.wait_recv()
        whole = wy[0].astype(F32)
        for d in range(1, NY):
            whole = whole + wy[d].astype(F32)
        wres[place.z] = whole.astype(BF16)
        yield from ring_gather(
            net, NZ, place.at_z(1), place.at_z(-1), lambda k: wres.at[place.zi(k)], UNIT_HALVES
        )
        done = result(wres, 0)
        yield
        for copy in done:
            copy.wait()

    def sum_y_first():
        total = wgrad.at[1]
        yield from ring_scatter(
            net, NY, place.at_y(1), place.at_y(-1), lambda k: total.at[:, place.yi(k)], nothing,
            lambda s: vyl.at[s], lambda s: vyr.at[s], ZBLOCK_HALVES,
        )
        yield from ring_scatter(
            net, NZ, place.at_z(1), place.at_z(-1), lambda k: total.at[place.zi(k), y], nothing,
            lambda s: vzl.at[s], lambda s: vzr.at[s], WROW_HALVES,
        )
        vres[place.z, y] = total[place.z, y]
        yield from ring_gather(
            net, NZ, place.at_z(1), place.at_z(-1), lambda k: vres.at[place.zi(k), y], WROW_HALVES
        )
        yield from ring_gather(
            net, NY, place.at_y(1), place.at_y(-1), lambda k: vres.at[:, place.yi(k)], ZBLOCK_HALVES
        )
        done = result(vres, 1)
        yield
        for copy in done:
            copy.wait()

    def go(chain):
        return next(chain, chain) is not chain

    f = [fetch(p) for p in range(PARTS)]
    s = [give_back(p) for p in range(PARTS)]
    first, second = sum_z_first(), sum_y_first()
    go(f[0])
    go(f[0])
    go(f[1])
    go(f[0])
    go(f[1])
    go(f[2])
    go(f[0])
    for copy in loads:
        copy.wait()
    attend(0, 0)
    go(f[1])
    go(f[2])
    attend(0, 1)
    slab_term(0)
    go(s[0])
    go(f[1])
    attend(1, 0)
    go(f[2])
    go(s[0])
    attend(1, 1)
    slab_term(1)
    go(s[1])
    go(f[2])
    attend(2, 0)
    go(s[0])
    go(s[1])
    weight_term(0)
    go(first)
    attend(2, 1)
    slab_term(2)
    go(s[2])
    go(s[0])
    go(s[1])
    go(first)
    go(s[2])
    weight_term(1)
    go(second)
    go(s[1])
    go(first)
    go(s[2])
    go(second)
    go(first)
    go(s[2])
    slabs = sum_slabs()
    live = [slabs, second, first]
    while live:
        live = [chain for chain in live if go(chain)]
    net.finish()


def fused(meta, states, queries, out_grad, key_weight, value_weight):
    slab = (TOK, E)
    block = (WROWS, HD)
    scratch = [
        pltpu.VMEM((NY, 8, 128), jnp.int32),
        pltpu.SMEM((NY, 8, 128), jnp.int32),
        pltpu.VMEM(queries.shape, BF16),
        pltpu.VMEM(out_grad.shape, BF16),
        pltpu.VMEM((2, E, LOCAL), BF16),
        pltpu.VMEM((NZ, ROWS) + slab, BF16),
        pltpu.VMEM((PARTS, 3, SPART) + slab, BF16),
        pltpu.VMEM((PARTS, 3, SPART) + slab, BF16),
        pltpu.VMEM((GROUPS, SLOTS) + slab, BF16),
        pltpu.VMEM((E, PARTS * PROWS), BF16),
        pltpu.VMEM((2, PARTS, GROUPS, SPART, TOK, LOCAL), BF16),
        pltpu.VMEM((GROUPS, SLOTS) + slab, BF16),
        pltpu.VMEM((PARTS, NX, SPART) + slab, BF16),
        pltpu.VMEM((PARTS, 3, SPART) + slab, BF16),
        pltpu.VMEM((NY, SLOTS) + slab, BF16),
        pltpu.VMEM((NZ, ROWS) + slab, BF16),
        pltpu.VMEM((NZ // 2, ROWS) + slab, BF16),
        pltpu.VMEM((NZ // 2, ROWS) + slab, BF16),
        pltpu.VMEM((2, NZ, UNITS) + block, BF16),
        pltpu.VMEM((NZ // 2, UNITS) + block, BF16),
        pltpu.VMEM((NZ // 2, UNITS) + block, BF16),
        pltpu.VMEM((NY, UNITS) + block, BF16),
        pltpu.VMEM((NZ, UNITS) + block, BF16),
        pltpu.VMEM((NY // 2, NZ) + block, BF16),
        pltpu.VMEM((NY // 2, NZ) + block, BF16),
        pltpu.VMEM((NZ // 2,) + block, BF16),
        pltpu.VMEM((NZ // 2,) + block, BF16),
        pltpu.VMEM((NZ, UNITS) + block, BF16),
        pltpu.SemaphoreType.DMA((COPIES,)),
        pltpu.SemaphoreType.DMA((COPIES,)),
        pltpu.SemaphoreType.DMA((LOCALS,)),
    ]
    anywhere = pl.BlockSpec(memory_space=pl.ANY)
    vmem = pl.BlockSpec(memory_space=pltpu.VMEM)
    wshape = jax.ShapeDtypeStruct((NZ, WROWS, LOCAL), BF16)
    return pl.pallas_call(
        kernel,
        out_shape=[
            jax.ShapeDtypeStruct(queries.shape, BF16),
            jax.ShapeDtypeStruct(queries.shape, BF16),
            jax.ShapeDtypeStruct(states.shape, F32),
            wshape,
            wshape,
        ],
        in_specs=[vmem] + [anywhere] * 5,
        out_specs=[vmem] * 3 + [anywhere] * 2,
        scratch_shapes=scratch,
        compiler_params=pltpu.CompilerParams(
            collective_id=0, has_side_effects=True, vmem_limit_bytes=VMEM_LIMIT
        ),
        name="retrieve",
    )(meta, states, queries, out_grad, key_weight, value_weight)


def describe(nbr_shard, nbr_row):
    spans, count = nbr_shard.shape
    slots = jnp.arange(SLOTS, dtype=jnp.int32)
    spot = jnp.arange(count, dtype=jnp.int32)[:, None] + count * jnp.arange(spans, dtype=jnp.int32)[None, :]
    pick = (spot[:, :, None] == slots[None, None, :]).astype(jnp.int32)
    owners = jnp.sum(nbr_shard.T[:, :, None] * pick, axis=(0, 1))
    rows = jnp.sum(nbr_row.T[:, :, None] * pick, axis=(0, 1))
    entry = (owners // NY) * ROWS + rows
    column = lax.rem(owners, NY)
    same = jnp.logical_and(owners[:, None] == owners[None, :], slots[:, None] > slots[None, :])
    key = owners * 2 + jnp.sum(same.astype(jnp.int32), axis=1)
    hit = key[:, None] == jnp.arange(128, dtype=jnp.int32)[None, :]
    slot_of = jnp.sum(jnp.where(hit, slots[:, None], 0), axis=0)
    row_of = jnp.sum(jnp.where(hit, rows[:, None] + 1, 0), axis=0) - 1
    pad = (0, 128 - SLOTS)
    blank = jnp.zeros((128,), jnp.int32)
    return jnp.stack([jnp.pad(entry, pad), jnp.pad(column, pad), slot_of, row_of] + [blank] * 4)


def body(queries, states, key_weight, value_weight, nbr_shard, nbr_row, out_grad):
    attended, query_grad, state_total, ktotal, vtotal = fused(
        describe(nbr_shard, nbr_row), states, queries, out_grad, key_weight, value_weight
    )
    return (
        attended, query_grad, state_total,
        ktotal.reshape(E, LOCAL).astype(F32), vtotal.reshape(E, LOCAL).astype(F32),
    )


def solution(mesh):
    placed = (
        P("dp", "mp"),
        P("dp", "mp", None),
        P(None, "mp"),
        P(None, "mp"),
        P("dp", None),
        P("dp", None),
        P("dp", "mp"),
    )
    return jax.shard_map(
        body,
        mesh=mesh,
        in_specs=placed,
        out_specs=(P("dp", "mp"), P("dp", "mp"), P("dp", "mp", None), P(None, "mp"), P(None, "mp")),
        check_vma=False,
    )
```

time: 405 us -> 158 us (0.39)
  waiting for transfers between devices: 265 us -> 0 us
  Pallas kernels: 0 us -> 148 us
  matrix products: 40.6 us -> 0 us
  local copies, waits for them, and re-layouts: 43.4 us -> 4.42 us
  blocking collectives: 21 us -> 0 us
  starting transfers between devices: 14.3 us -> 0 us
  between operations: 14.1 us -> 0.68 us
    pallas_call x0 -> x1, Pallas kernels: none -> 148 us  [fused(): pl.pallas_call(kernel, out_shape=[jax.ShapeDtypeStruct(queries.shape, BF1...]
    psum x1 -> x0, waiting for transfers between devices: 123 us -> none  [body(): key_total, value_total = lax.psum((key_wgrad, value_wgrad), 'dp')]
    all_to_all x2 -> x0, waiting for transfers between devices: 85.6 us -> none  [the longest x1 43.8 us: body(): lax.all_to_all(slab_rows, 'dp', split_axis=0, concat_axis=0, tiled=True)]
    dot_general x15 -> x0, matrix products: 40.6 us -> none  [the longest x1 5.83 us: body(): jnp.einsum('chqk,cqhd->ckhd', probs_low, grad_heads, preferred_element_ty...]
    reduce_scatter x1 -> x0, waiting for transfers between devices: 32.5 us -> none  [body(): lax.psum_scatter(state_term.astype(jnp.bfloat16), 'mp', scatter_dimension...]
    all_gather x1 -> x0, waiting for transfers between devices: 24.6 us -> none  [body(): gathered = lax.all_gather(picked, 'mp', axis=1, tiled=True)]
    all_to_all x1 -> x0, blocking collectives: 21 us -> none  [body(): lax.all_to_all(asked_rows, 'dp', split_axis=0, concat_axis=0, tiled=True)]
    reshape x9 -> x0, local copies, waits for them, and re-layouts: 20 us -> none  [the longest x2 8.78 us: body(): outgoing.astype(jnp.bfloat16).reshape(shards, capacity, slab_len, enc_width)]
  transfers between devices with their start and end apart: 5 -> 0, of which waited for: 5 -> 0; matrix products, arithmetic and copies ran while one was open for 7% -> 0% of each run, Pallas kernels for 0% -> 0%
where the time goes in v2:
time: 158 us
  Pallas kernels  148 us (94%)
  other arithmetic  4.75 us (3%)
  local copies, waits for them, and re-layouts  4.42 us (3%)
    pallas_call x1, Pallas kernels, fused(): pl.pallas_call(kernel, out_shape=[jax.ShapeDtypeStruct(queries.shape, BF1...  148 us

profile of v2, /device:TPU:2, one launch (start us, length us, event | category | flops | bytes accessed | tf_op | source)
XLA Modules:
  0.0 157.7 jit_solution(9741075482800663050)
XLA Ops:
  0.6 0.1 iota_add_fusion
  0.7 0.8 copy.12
  1.5 0.8 copy.13
  2.2 0.1 select_reduce_fusion.3
  2.3 0.2 convert_reduce_fusion
  2.6 0.1 select_reduce_fusion
  2.7 0.6 stack.20.meta_in
  3.3 147.8 %retrieve.1 = (bf16[384,512]{1,0:T(8,128)(2,1)}, bf16[384,512]{1,0:T(8,128)(2,1)}, f32[8,16,896]{2,1,0:T(8,128)}, bf16[8,112,512]{2,1,0:T(8,128)(2,1)}, bf16[8,112,512]{2,1,0:T(8,128)(2,1)}) custom-call(s32[8,128]{1,0:T(8,128)} %stack.20.meta_in, bf16[8,16,896]{2,1,0:T(8,128)(2,1)} %states.1, bf16[384,512]{1,0:T(8,128)(2,1)} %queries.1, ...), custom_call_target="tpu_custom_call" | custom-call | tf_op jit(solution)/shard_map/retrieve/pallas_call | solution.py:492
  151.1 0.0 copy-start
  151.1 2.7 %bitcast_convert_fusion.1 = f32[896,512]{1,0:T(8,128)} fusion(bf16[8,112,512]{2,1,0:T(8,128)(2,1)} %get-tuple-element.13), kind=kLoop, calls=%fused_computation.1 | loop fusion | flops 458752 | bytes 2752512 | tf_op jit(solution)/shard_map/convert_element_type | solution.py:536
  153.9 0.0 copy-done
  153.9 0.0 copy-start.3
  153.9 0.0 copy-start.2
  153.9 0.0 copy-start.1
  153.9 1.5 bitcast_convert_fusion
  155.4 0.0 copy-done.3
  155.4 0.7 copy.17
  156.2 0.0 copy-done.2
  156.2 0.7 copy.18
  156.9 0.0 copy-done.1
  156.9 0.8 copy.19
  (5 shorter events, 0.0 us)
Async XLA Ops:
  151.1 2.8 %copy-start = (bf16[8,112,512]{2,1,0:T(8,128)(2,1)S(1)}, bf16[8,112,512]{2,1,0:T(8,128)(2,1)}, u32[]{:S(2)}) copy-start(bf16[8,112,512]{2,1,0:T(8,128)(2,1)} %get-tuple-element.14) | copy-start | bytes 2752516
  153.9 1.6 copy-start.3
  153.9 2.3 %copy-start.2 = (bf16[384,512]{1,0:T(8,128)(2,1)S(1)}, bf16[384,512]{1,0:T(8,128)(2,1)}, u32[]{:S(2)}) copy-start(bf16[384,512]{1,0:T(8,128)(2,1)} %get-tuple-element.31) | copy-start | bytes 1179652
  153.9 3.0 %copy-start.1 = (f32[8,16,896]{2,1,0:T(8,128)S(1)}, f32[8,16,896]{2,1,0:T(8,128)}, u32[]{:S(2)}) copy-start(f32[8,16,896]{2,1,0:T(8,128)} %get-tuple-element.32) | copy-start | bytes 1376260

commit v3 on v2

--- a/solution.py
+++ b/solution.py
@@ -1,3 +1,5 @@
+import functools
+
 import jax
 import jax.numpy as jnp
 from jax import lax
@@ -161,17 +163,23 @@
 ROW_HALVES = ((0, ROWS // 2), (ROWS // 2, ROWS // 2))
 SPAN_LEN = 64
 LOCAL = 512
-PARTS = 3
-SPART = SLOTS // PARTS
-PROWS = GROUPS * SPART * TOK
+NLEN = GROUPS * TOK
+PARTS = ((0, 4), (4, 4), (8, 4))
 WROWS = E // NZ
 UNITS = 4
+Y_FIRST = 1
 UNIT_HALVES = ((0, UNITS // 2), (UNITS // 2, UNITS // 2))
 ZBLOCK_HALVES = ((0, NZ // 2), (NZ // 2, NZ // 2))
 WROW_HALVES = ((0, 64), (64, WROWS - 64))
 COPIES = 160
 LOCALS = 32
 AROUND = (1, -1, 2)
+PLAN = (
+    "f0", "load", "f1", "f2", "f0", "f1", "f0", "f2", "f0", "a00", "a01", "f1", "f2", "t0", "f1", "a10", "f2",
+    "a20", "w0", "B", "a21", "s0", "a11", "s0", "B", "t1", "s1", "w1", "A", "s1", "B", "t2", "s2", "s0", "A",
+    "s2", "B", "s1", "B", "A", "s0", "B", "s2", "A", "B", "s1", "A", "B", "s2", "Z", "B", "A", "Z", "B", "A",
+    "Z", "B", "A", "Z", "B", "A", "B", "B", "Z", "A", "A",
+)
 
 
 def mm(a, b, dims):
@@ -182,7 +190,7 @@
     meta_in, states, queries, out_grad, key_weight, value_weight,
     att, qg, state_out, kout, vout,
     meta_v, meta_s, q, g, weights, zbuf, ysend, yrecv, rows, rows_t, grads, terms, theirs, xrecv,
-    ybuf, share, zl, zr, wgrad, wfl, wfr, wy, wres, vyl, vyr, vzl, vzr, vres,
+    ybuf, share, zl, zr, wgrad, wfl, wfr, wy, wres, vyl, vyr, vzl, vzr, vres, wide,
     send_sems, recv_sems, local_sems,
 ):
     place = Place()
@@ -213,7 +221,9 @@
     to_smem.wait()
 
     def fetch(p):
-        at = pl.ds(p * SPART, SPART)
+        first, count = PARTS[p]
+        at = pl.ds(first, count)
+        slots = range(first, first + count)
 
         def held(k, j):
             entry = meta_s[place.yi(k), 0, j]
@@ -221,17 +231,17 @@
 
         copies = []
         for n, k in enumerate(AROUND):
-            for j in range(SPART):
-                ysend[p, n, j] = held(k, p * SPART + j)
-            copies.append(net.send(ysend.at[p, n], yrecv.at[p, n], place.at_y(k)))
+            for j in slots:
+                ysend[n, j] = held(k, j)
+            copies.append(net.send(ysend.at[n, at], yrecv.at[n, at], place.at_y(k)))
         yield
         for copy in copies:
             copy.wait_recv()
-        for j in range(SPART):
-            column = meta_s[y, 1, p * SPART + j]
-            value = lax.select(column == place.yi(-1), yrecv[p, 0, j], yrecv[p, 1, j])
-            value = lax.select(column == place.yi(2), yrecv[p, 2, j], value)
-            rows[mp, p * SPART + j] = lax.select(column == y, held(0, p * SPART + j), value)
+        for j in slots:
+            column = meta_s[y, 1, j]
+            value = lax.select(column == place.yi(-1), yrecv[0, j], yrecv[1, j])
+            value = lax.select(column == place.yi(2), yrecv[2, j], value)
+            rows[mp, j] = lax.select(column == y, held(0, j), value)
 
         def block(k):
             return rows.at[place.xi(k) * 2 + place.core, at]
@@ -248,14 +258,15 @@
 
     def attend(p, i):
         scale = 1.0 / HD**0.5
-        at = pl.ds(p * SPART, SPART)
-        part_rows = rows[:, at].reshape(PROWS, E)
-        if i == 0:
-            rows_t[:, pl.ds(p * PROWS, PROWS)] = part_rows.T
-        both = mm(part_rows, weights[i], ((1,), (0,))).astype(BF16).reshape(GROUPS, SPART, TOK, LOCAL)
-        for c in range(SPART // 2):
-            span_both = both[:, 2 * c:2 * c + 2].reshape(2 * GROUPS * TOK, LOCAL)
-            span = pl.ds((p * (SPART // 2) + c) * SPAN_LEN, SPAN_LEN)
+        first, count = PARTS[p]
+        part_rows = jnp.concatenate([rows[:, j].reshape(NLEN, E) for j in range(first, first + count)], axis=0)
+        if i == Y_FIRST:
+            rows_t[:, pl.ds(first * NLEN, count * NLEN)] = part_rows.T
+        both = mm(part_rows, weights[i], ((1,), (0,))).astype(BF16)
+        for c in range(count // 2):
+            span_both = both[2 * c * NLEN:2 * (c + 1) * NLEN]
+            span = pl.ds((first // 2 + c) * SPAN_LEN, SPAN_LEN)
+            span_rows = pl.ds((first + 2 * c) * NLEN, 2 * NLEN)
             for h in range(2):
                 cols = pl.ds((2 * i + h) * HD, HD)
                 qh, gh = q[span, cols], g[span, cols]
@@ -271,33 +282,30 @@
                 dot = jnp.sum(probs * pgrad, axis=-1, keepdims=True)
                 sgrad = (scale * probs * (pgrad - dot)).astype(BF16)
                 qg[span, cols] = mm(sgrad, kh, ((1,), (0,))).astype(BF16)
-                shape = (GROUPS, 2, TOK, HD)
-                pair = pl.ds(2 * c, 2)
-                grads[i, p, :, pair, :, pl.ds(h * HD, HD)] = (
-                    mm(sgrad, qh, ((0,), (0,))).astype(BF16).reshape(shape)
-                )
-                grads[i, p, :, pair, :, pl.ds(half + h * HD, HD)] = (
-                    mm(low, gh, ((0,), (0,))).astype(BF16).reshape(shape)
-                )
+                grads[i, span_rows, pl.ds(h * HD, HD)] = mm(sgrad, qh, ((0,), (0,))).astype(BF16)
+                grads[i, span_rows, pl.ds(half + h * HD, HD)] = mm(low, gh, ((0,), (0,))).astype(BF16)
 
     def slab_term(p):
+        first, count = PARTS[p]
         total = None
         for i in range(2):
-            term = mm(grads[i, p].reshape(PROWS, LOCAL), weights[i], ((1,), (1,)))
+            term = mm(grads[i, pl.ds(first * NLEN, count * NLEN)], weights[i], ((1,), (1,)))
             total = term if total is None else total + term
-        terms[:, pl.ds(p * SPART, SPART)] = total.astype(BF16).reshape(GROUPS, SPART, TOK, E)
+        total = total.astype(BF16)
+        for j in range(count):
+            terms[:, first + j] = total[j * NLEN:(j + 1) * NLEN].reshape(GROUPS, TOK, E)
 
     def weight_term(i):
-        total = mm(rows_t[...], grads[i].reshape(PARTS * PROWS, LOCAL), ((1,), (0,))).astype(BF16)
+        total = mm(rows_t[...], grads[i], ((1,), (0,))).astype(BF16)
         for z in range(NZ):
             for u in range(UNITS):
                 wgrad[i, z, u] = total[z * WROWS:(z + 1) * WROWS, u * HD:(u + 1) * HD]
 
     def give_back(p):
-        at = pl.ds(p * SPART, SPART)
+        at = pl.ds(*PARTS[p])
         order = AROUND + (0,)
         copies = [
-            net.send(terms.at[place.xi(k) * 2 + (1 - place.core), at], theirs.at[p, n], place.sibling())
+            net.send(terms.at[place.xi(k) * 2 + (1 - place.core), at], theirs.at[n, at], place.sibling())
             for n, k in enumerate(order)
         ]
         yield
@@ -305,15 +313,15 @@
         for n, k in enumerate(order):
             copies[n].wait_recv()
             block = terms.at[place.xi(k) * 2 + place.core, at]
-            add_into(block, theirs.at[p, n])
+            add_into(block, theirs.at[n, at])
             if k != 0:
-                crossing.append(net.send(block, xrecv.at[p, n], place.at_x(k)))
+                crossing.append(net.send(block, xrecv.at[n, at], place.at_x(k)))
         yield
         for copy in crossing:
             copy.wait_recv()
         total = terms[mp, at].astype(F32)
         for n in range(3):
-            total = total + xrecv[p, n].astype(F32)
+            total = total + xrecv[n, at].astype(F32)
         ybuf[y, at] = total.astype(BF16)
         copies = [net.send(ybuf.at[y, at], ybuf.at[y, at], place.at_y(k)) for k in AROUND]
         yield
@@ -344,10 +352,11 @@
         state_out[...] = share[0].astype(F32)
 
     def result(res, i):
-        return [
-            net.local(res.at[:, u], out.at[:, :, pl.ds((2 * i + u % 2) * HD, HD)])
-            for u, out in enumerate((kout, kout, vout, vout))
-        ]
+        copies = []
+        for u, out in enumerate((kout, kout, vout, vout)):
+            wide[i, u] = res[:, u].astype(F32)
+            copies.append(net.local(wide.at[i, u], out.at[:, :, pl.ds((2 * i + u % 2) * HD, HD)]))
+        return copies
 
     def sum_z_first():
         total = wgrad.at[0]
@@ -394,59 +403,27 @@
         for copy in done:
             copy.wait()
 
-    def go(chain):
-        return next(chain, chain) is not chain
-
-    f = [fetch(p) for p in range(PARTS)]
-    s = [give_back(p) for p in range(PARTS)]
-    first, second = sum_z_first(), sum_y_first()
-    go(f[0])
-    go(f[0])
-    go(f[1])
-    go(f[0])
-    go(f[1])
-    go(f[2])
-    go(f[0])
-    for copy in loads:
-        copy.wait()
-    attend(0, 0)
-    go(f[1])
-    go(f[2])
-    attend(0, 1)
-    slab_term(0)
-    go(s[0])
-    go(f[1])
-    attend(1, 0)
-    go(f[2])
-    go(s[0])
-    attend(1, 1)
-    slab_term(1)
-    go(s[1])
-    go(f[2])
-    attend(2, 0)
-    go(s[0])
-    go(s[1])
-    weight_term(0)
-    go(first)
-    attend(2, 1)
-    slab_term(2)
-    go(s[2])
-    go(s[0])
-    go(s[1])
-    go(first)
-    go(s[2])
-    weight_term(1)
-    go(second)
-    go(s[1])
-    go(first)
-    go(s[2])
-    go(second)
-    go(first)
-    go(s[2])
-    slabs = sum_slabs()
-    live = [slabs, second, first]
-    while live:
-        live = [chain for chain in live if go(chain)]
+    chains = {"A": sum_z_first(), "B": sum_y_first(), "Z": sum_slabs()}
+
+    def load():
+        for copy in loads:
+            copy.wait()
+
+    work = {"load": load, "w0": lambda: weight_term(Y_FIRST), "w1": lambda: weight_term(1 - Y_FIRST)}
+    for p in range(len(PARTS)):
+        chains[f"f{p}"] = fetch(p)
+        chains[f"s{p}"] = give_back(p)
+        work[f"t{p}"] = functools.partial(slab_term, p)
+        work[f"a{p}0"] = functools.partial(attend, p, Y_FIRST)
+        work[f"a{p}1"] = functools.partial(attend, p, 1 - Y_FIRST)
+    for name in PLAN:
+        if name in work:
+            work[name]()
+        else:
+            next(chains[name], None)
+    for chain in chains.values():
+        for _ in chain:
+            pass
     net.finish()
 
 
@@ -460,14 +437,14 @@
         pltpu.VMEM(out_grad.shape, BF16),
         pltpu.VMEM((2, E, LOCAL), BF16),
         pltpu.VMEM((NZ, ROWS) + slab, BF16),
-        pltpu.VMEM((PARTS, 3, SPART) + slab, BF16),
-        pltpu.VMEM((PARTS, 3, SPART) + slab, BF16),
+        pltpu.VMEM((len(AROUND), SLOTS) + slab, BF16),
+        pltpu.VMEM((len(AROUND), SLOTS) + slab, BF16),
         pltpu.VMEM((GROUPS, SLOTS) + slab, BF16),
-        pltpu.VMEM((E, PARTS * PROWS), BF16),
-        pltpu.VMEM((2, PARTS, GROUPS, SPART, TOK, LOCAL), BF16),
+        pltpu.VMEM((E, SLOTS * NLEN), BF16),
+        pltpu.VMEM((2, SLOTS * NLEN, LOCAL), BF16),
         pltpu.VMEM((GROUPS, SLOTS) + slab, BF16),
-        pltpu.VMEM((PARTS, NX, SPART) + slab, BF16),
-        pltpu.VMEM((PARTS, 3, SPART) + slab, BF16),
+        pltpu.VMEM((NX, SLOTS) + slab, BF16),
+        pltpu.VMEM((len(AROUND), SLOTS) + slab, BF16),
         pltpu.VMEM((NY, SLOTS) + slab, BF16),
         pltpu.VMEM((NZ, ROWS) + slab, BF16),
         pltpu.VMEM((NZ // 2, ROWS) + slab, BF16),
@@ -482,13 +459,14 @@
         pltpu.VMEM((NZ // 2,) + block, BF16),
         pltpu.VMEM((NZ // 2,) + block, BF16),
         pltpu.VMEM((NZ, UNITS) + block, BF16),
+        pltpu.VMEM((2, UNITS, NZ) + block, F32),
         pltpu.SemaphoreType.DMA((COPIES,)),
         pltpu.SemaphoreType.DMA((COPIES,)),
         pltpu.SemaphoreType.DMA((LOCALS,)),
     ]
     anywhere = pl.BlockSpec(memory_space=pl.ANY)
     vmem = pl.BlockSpec(memory_space=pltpu.VMEM)
-    wshape = jax.ShapeDtypeStruct((NZ, WROWS, LOCAL), BF16)
+    wshape = jax.ShapeDtypeStruct((NZ, WROWS, LOCAL), F32)
     return pl.pallas_call(
         kernel,
         out_shape=[
@@ -533,7 +511,7 @@
     )
     return (
         attended, query_grad, state_total,
-        ktotal.reshape(E, LOCAL).astype(F32), vtotal.reshape(E, LOCAL).astype(F32),
+        ktotal.reshape(E, LOCAL), vtotal.reshape(E, LOCAL),
     )
 
 

time: 158 us -> 140 us (0.89)
  Pallas kernels: 148 us -> 127 us
  local copies, waits for them, and re-layouts: 4.42 us -> 11 us
  other arithmetic: 4.75 us -> 0.46 us
    pallas_call x1, Pallas kernels: 148 us -> 127 us  [fused(): pl.pallas_call(kernel, out_shape=[jax.ShapeDtypeStruct(queries.shape, BF1...]
    unnamed x11 -> x9, local copies, waits for them, and re-layouts: 2.27 us -> 8.87 us
    convert_element_type x2 -> x0, other arithmetic: 4.28 us -> none  [the longest x1 2.74 us: body(): ktotal.reshape(E, LOCAL).astype(F32)]
where the time goes in v3:
time: 140 us; the launch traced here: 139 us
  Pallas kernels  127 us (91%)
  local copies, waits for them, and re-layouts  11 us (8%)
    pallas_call x1, Pallas kernels, fused(): pl.pallas_call(kernel, out_shape=[jax.ShapeDtypeStruct(queries.shape, BF1...  127 us
    unnamed x9, local copies, waits for them, and re-layouts  8.87 us

profile of v3, /device:TPU:2, one launch (start us, length us, event | category | flops | bytes accessed | tf_op | source)
XLA Modules:
  0.0 139.4 jit_solution(14141212311281656728)
XLA Ops:
  0.6 0.1 iota_add_fusion
  0.7 0.8 copy.12
  1.5 0.8 copy.13
  2.2 0.1 select_reduce_fusion.3
  2.3 0.2 convert_reduce_fusion
  2.6 0.1 select_reduce_fusion
  2.7 0.6 stack.20.meta_in
  3.3 127.2 %retrieve.1 = (bf16[384,512]{1,0:T(8,128)(2,1)}, bf16[384,512]{1,0:T(8,128)(2,1)}, f32[8,16,896]{2,1,0:T(8,128)}, f32[8,112,512]{2,1,0:T(8,128)}, f32[8,112,512]{2,1,0:T(8,128)}) custom-call(s32[8,128]{1,0:T(8,128)} %stack.20.meta_in, bf16[8,16,896]{2,1,0:T(8,128)(2,1)} %states.1, bf16[384,512]{1,0:T(8,128)(2,1)} %queries.1, bf16[384,512]{1,0:T(8,128)(2,1)} %out_grad.1, ...), custom_call_target="tpu_custom_call" | custom-call | tf_op jit(solution)/shard_map/retrieve/pallas_call | solution.py:470
  130.5 0.0 copy-start.1
  130.5 1.9 %copy.19 = bf16[384,512]{1,0:T(8,128)(2,1)} copy(bf16[384,512]{1,0:T(8,128)(2,1)} %get-tuple-element.30) | data formatting | bytes 786432
  132.4 1.8 %copy.20 = bf16[384,512]{1,0:T(8,128)(2,1)} copy(bf16[384,512]{1,0:T(8,128)(2,1)} %get-tuple-element.31) | data formatting | bytes 786432
  134.2 1.8 %copy.21 = f32[8,16,896]{2,1,0:T(8,128)} copy(f32[8,16,896]{2,1,0:T(8,128)} %get-tuple-element.32) | data formatting | bytes 917504
  136.0 0.0 copy-done.1
  136.0 0.0 copy-start
  136.0 1.2 copy.22
  137.2 0.9 copy-done
  138.2 1.2 copy.23
  (5 shorter events, 0.0 us)
Async XLA Ops:
  130.5 5.5 %copy-start.1 = (f32[8,112,512]{2,1,0:T(8,128)S(1)}, f32[8,112,512]{2,1,0:T(8,128)}, u32[]{:S(2)}) copy-start(f32[8,112,512]{2,1,0:T(8,128)} %get-tuple-element.13) | copy-start | bytes 5505028
  136.0 2.2 %copy-start = (f32[8,112,512]{2,1,0:T(8,128)S(1)}, f32[8,112,512]{2,1,0:T(8,128)}, u32[]{:S(2)}) copy-start(f32[8,112,512]{2,1,0:T(8,128)} %get-tuple-element.14) | copy-start | bytes 5505028

commit v4 on v3

--- a/solution.py
+++ b/solution.py
@@ -18,6 +18,7 @@
 TOK = 16
 E = 896
 VMEM_LIMIT = 56 * 1024 * 1024
+FINISH_STEPS = 4
 BF16 = jnp.bfloat16
 F32 = jnp.float32
 
@@ -164,7 +165,7 @@
 SPAN_LEN = 64
 LOCAL = 512
 NLEN = GROUPS * TOK
-PARTS = ((0, 4), (4, 4), (8, 4))
+PARTS = ((0, 4), (4, 4), (8, 2), (10, 2))
 WROWS = E // NZ
 UNITS = 4
 Y_FIRST = 1
@@ -175,10 +176,11 @@
 LOCALS = 32
 AROUND = (1, -1, 2)
 PLAN = (
-    "f0", "load", "f1", "f2", "f0", "f1", "f0", "f2", "f0", "a00", "a01", "f1", "f2", "t0", "f1", "a10", "f2",
-    "a20", "w0", "B", "a21", "s0", "a11", "s0", "B", "t1", "s1", "w1", "A", "s1", "B", "t2", "s2", "s0", "A",
-    "s2", "B", "s1", "B", "A", "s0", "B", "s2", "A", "B", "s1", "A", "B", "s2", "Z", "B", "A", "Z", "B", "A",
-    "Z", "B", "A", "Z", "B", "A", "B", "B", "Z", "A", "A",
+    "f2", "f3", "load", "f1", "f2", "f3", "f0", "f2", "f1", "f2", "a20", "f3", "a21", "t2", "f3", "s2", "f0",
+    "a30", "s2", "f1", "a31", "f1", "a10", "f0", "a11", "t1", "f0", "a00", "s1", "w0", "B", "s1", "a01", "w1",
+    "A", "t3", "s3", "B", "t0", "s0", "s3", "s1", "s2", "A", "s0", "B", "A", "s3", "B", "s0", "s1", "B", "A",
+    "B", "s2", "A", "s3", "B", "s0", "Z", "B", "A", "B", "Z", "B", "A", "Z", "B", "A", "Z", "B", "A", "B",
+    "B", "Z", "A", "A",
 )
 
 
@@ -190,7 +192,7 @@
     meta_in, states, queries, out_grad, key_weight, value_weight,
     att, qg, state_out, kout, vout,
     meta_v, meta_s, q, g, weights, zbuf, ysend, yrecv, rows, rows_t, grads, terms, theirs, xrecv,
-    ybuf, share, zl, zr, wgrad, wfl, wfr, wy, wres, vyl, vyr, vzl, vzr, vres, wide,
+    ybuf, share, zl, zr, wgrad, wfl, wfr, wy, wres, vyl, vyr, vzl, vzr, vres,
     send_sems, recv_sems, local_sems,
 ):
     place = Place()
@@ -352,11 +354,10 @@
         state_out[...] = share[0].astype(F32)
 
     def result(res, i):
-        copies = []
-        for u, out in enumerate((kout, kout, vout, vout)):
-            wide[i, u] = res[:, u].astype(F32)
-            copies.append(net.local(wide.at[i, u], out.at[:, :, pl.ds((2 * i + u % 2) * HD, HD)]))
-        return copies
+        return [
+            net.local(res.at[:, u], out.at[:, :, pl.ds((2 * i + u % 2) * HD, HD)])
+            for u, out in enumerate((kout, kout, vout, vout))
+        ]
 
     def sum_z_first():
         total = wgrad.at[0]
@@ -459,14 +460,13 @@
         pltpu.VMEM((NZ // 2,) + block, BF16),
         pltpu.VMEM((NZ // 2,) + block, BF16),
         pltpu.VMEM((NZ, UNITS) + block, BF16),
-        pltpu.VMEM((2, UNITS, NZ) + block, F32),
         pltpu.SemaphoreType.DMA((COPIES,)),
         pltpu.SemaphoreType.DMA((COPIES,)),
         pltpu.SemaphoreType.DMA((LOCALS,)),
     ]
     anywhere = pl.BlockSpec(memory_space=pl.ANY)
     vmem = pl.BlockSpec(memory_space=pltpu.VMEM)
-    wshape = jax.ShapeDtypeStruct((NZ, WROWS, LOCAL), F32)
+    wshape = jax.ShapeDtypeStruct((NZ, WROWS, LOCAL), BF16)
     return pl.pallas_call(
         kernel,
         out_shape=[
@@ -505,14 +505,34 @@
     return jnp.stack([jnp.pad(entry, pad), jnp.pad(column, pad), slot_of, row_of] + [blank] * 4)
 
 
+def finish_kernel(*refs):
+    count = len(refs) // 2
+    for source, target in zip(refs[:count], refs[count:]):
+        target[...] = source[...].astype(target.dtype)
+
+
+def finish(arrays, types, steps):
+    specs = []
+    for array in arrays:
+        rest = array.shape[1:]
+        specs.append(
+            pl.BlockSpec((array.shape[0] // steps,) + rest, lambda i, n=len(rest): (i,) + (0,) * n)
+        )
+    return pl.pallas_call(
+        finish_kernel,
+        grid=(steps,),
+        out_shape=[jax.ShapeDtypeStruct(array.shape, kind) for array, kind in zip(arrays, types)],
+        in_specs=specs,
+        out_specs=specs,
+        compiler_params=pltpu.CompilerParams(vmem_limit_bytes=VMEM_LIMIT),
+        name="finish",
+    )(*arrays)
+
+
 def body(queries, states, key_weight, value_weight, nbr_shard, nbr_row, out_grad):
-    attended, query_grad, state_total, ktotal, vtotal = fused(
-        describe(nbr_shard, nbr_row), states, queries, out_grad, key_weight, value_weight
-    )
-    return (
-        attended, query_grad, state_total,
-        ktotal.reshape(E, LOCAL), vtotal.reshape(E, LOCAL),
-    )
+    arrays = fused(describe(nbr_shard, nbr_row), states, queries, out_grad, key_weight, value_weight)
+    attended, query_grad, state_total, ktotal, vtotal = finish(arrays, (BF16, BF16, F32, F32, F32), FINISH_STEPS)
+    return attended, query_grad, state_total, ktotal.reshape(E, LOCAL), vtotal.reshape(E, LOCAL)
 
 
 def solution(mesh):

time: 140 us -> 132 us (0.943)
  local copies, waits for them, and re-layouts: 11 us -> 2.14 us
  Pallas kernels: 127 us -> 129 us
    unnamed x9 -> x0, local copies, waits for them, and re-layouts: 8.87 us -> none
    pallas_call x0 -> x1, Pallas kernels: none -> 4.67 us  [finish(): pl.pallas_call(finish_kernel, grid=(steps,), out_shape=[jax.ShapeDtypeStr...]
    pallas_call x1, Pallas kernels: 127 us -> 124 us  [fused(): pl.pallas_call(kernel, out_shape=[jax.ShapeDtypeStruct(queries.shape, BF1...]
where the time goes in v4:
time: 132 us
  Pallas kernels  129 us (98%)
  local copies, waits for them, and re-layouts  2.14 us (2%)
    pallas_call x1, Pallas kernels, fused(): pl.pallas_call(kernel, out_shape=[jax.ShapeDtypeStruct(queries.shape, BF1...  124 us
    pallas_call x1, Pallas kernels, finish(): pl.pallas_call(finish_kernel, grid=(steps,), out_shape=[jax.ShapeDtypeStr...  4.67 us

profile of v4, /device:TPU:2, one launch (start us, length us, event | category | flops | bytes accessed | tf_op | source)
XLA Modules:
  0.0 131.8 jit_solution(2737688779415899218)
XLA Ops:
  0.6 0.1 iota_add_fusion
  0.7 0.8 copy.12
  1.5 0.8 copy.13
  2.2 0.1 select_reduce_fusion.3
  2.3 0.2 convert_reduce_fusion
  2.6 0.1 select_reduce_fusion
  2.7 0.6 stack.20.meta_in
  3.3 123.9 %retrieve.1 = (bf16[384,512]{1,0:T(8,128)(2,1)}, bf16[384,512]{1,0:T(8,128)(2,1)}, f32[8,16,896]{2,1,0:T(8,128)}, bf16[8,112,512]{2,1,0:T(8,128)(2,1)}, bf16[8,112,512]{2,1,0:T(8,128)(2,1)}) custom-call(s32[8,128]{1,0:T(8,128)} %stack.20.meta_in, bf16[8,16,896]{2,1,0:T(8,128)(2,1)} %states.1, bf16[384,512]{1,0:T(8,128)(2,1)} %queries.1, ...), custom_call_target="tpu_custom_call" | custom-call | tf_op jit(solution)/shard_map/retrieve/pallas_call | solution.py:470
  127.1 4.7 %finish.1 = (bf16[384,512]{1,0:T(8,128)(2,1)}, bf16[384,512]{1,0:T(8,128)(2,1)}, f32[8,16,896]{2,1,0:T(8,128)}, f32[8,112,512]{2,1,0:T(8,128)}, f32[8,112,512]{2,1,0:T(8,128)}) custom-call(bf16[384,512]{1,0:T(8,128)(2,1)} %get-tuple-element.15.refs_0_, bf16[384,512]{1,0:T(8,128)(2,1)} %get-tuple-element.16.refs_1_, f32[8,16,896]{2,1,0:T(8,128)} %get-tuple-element.17.refs_2_, ...), custom_call_target="tpu_custom_call" | custom-call | tf_op jit(solution)/shard_map/finish/pallas_call | solution.py:521
  (5 shorter events, 0.0 us)

commit v5 on v4

--- a/solution.py
+++ b/solution.py
@@ -18,7 +18,7 @@
 TOK = 16
 E = 896
 VMEM_LIMIT = 56 * 1024 * 1024
-FINISH_STEPS = 4
+FINISH_STEPS = 2
 BF16 = jnp.bfloat16
 F32 = jnp.float32
 
@@ -277,7 +277,7 @@
                 scores = mm(qh, kh, ((1,), (1,))) * scale
                 top = jnp.max(scores, axis=-1, keepdims=True)
                 grown = jnp.exp(scores - top)
-                probs = grown / jnp.sum(grown, axis=-1, keepdims=True)
+                probs = grown * (1.0 / jnp.sum(grown, axis=-1, keepdims=True))
                 low = probs.astype(BF16)
                 att[span, cols] = mm(low, vh, ((1,), (0,))).astype(BF16)
                 pgrad = mm(gh, vh, ((1,), (1,)))

time: 132 us -> 131 us (level)
  no operation moved by 1% of the time
where the time goes in v5:
time: 131 us
  Pallas kernels  128 us (98%)
  local copies, waits for them, and re-layouts  2.14 us (2%)
    pallas_call x1, Pallas kernels, fused(): pl.pallas_call(kernel, out_shape=[jax.ShapeDtypeStruct(queries.shape, BF1...  124 us
    pallas_call x1, Pallas kernels, finish(): pl.pallas_call(finish_kernel, grid=(steps,), out_shape=[jax.ShapeDtypeStr...  3.83 us

profile of v5, /device:TPU:2, one launch (start us, length us, event | category | flops | bytes accessed | tf_op | source)
XLA Modules:
  0.0 131.0 jit_solution(7745691014215252554)
XLA Ops:
  0.6 0.1 iota_add_fusion
  0.7 0.8 copy.12
  1.5 0.8 copy.13
  2.2 0.1 select_reduce_fusion.3
  2.3 0.2 convert_reduce_fusion
  2.6 0.1 select_reduce_fusion
  2.7 0.6 stack.20.meta_in
  3.3 123.9 %retrieve.1 = (bf16[384,512]{1,0:T(8,128)(2,1)}, bf16[384,512]{1,0:T(8,128)(2,1)}, f32[8,16,896]{2,1,0:T(8,128)}, bf16[8,112,512]{2,1,0:T(8,128)(2,1)}, bf16[8,112,512]{2,1,0:T(8,128)(2,1)}) custom-call(s32[8,128]{1,0:T(8,128)} %stack.20.meta_in, bf16[8,16,896]{2,1,0:T(8,128)(2,1)} %states.1, bf16[384,512]{1,0:T(8,128)(2,1)} %queries.1, ...), custom_call_target="tpu_custom_call" | custom-call | tf_op jit(solution)/shard_map/retrieve/pallas_call | solution.py:470
  127.1 3.8 %finish.1 = (bf16[384,512]{1,0:T(8,128)(2,1)}, bf16[384,512]{1,0:T(8,128)(2,1)}, f32[8,16,896]{2,1,0:T(8,128)}, f32[8,112,512]{2,1,0:T(8,128)}, f32[8,112,512]{2,1,0:T(8,128)}) custom-call(bf16[384,512]{1,0:T(8,128)(2,1)} %get-tuple-element.15.refs_0_, bf16[384,512]{1,0:T(8,128)(2,1)} %get-tuple-element.16.refs_1_, f32[8,16,896]{2,1,0:T(8,128)} %get-tuple-element.17.refs_2_, ...), custom_call_target="tpu_custom_call" | custom-call | tf_op jit(solution)/shard_map/finish/pallas_call | solution.py:521
  (5 shorter events, 0.0 us)
